TPU v7x, 512 devices: a whole 4x8x8 slice. The times are simulated.
512 devices in a mesh: azi: 16 (over y_hi, x), ra: 32 (over y_lo, z, core).
Axes of the slice: x: 4, y: 8 (y_hi: 4, y_lo: 2; y = y_hi * 2 + y_lo), z: 8, core: 2. Of those that a mesh axis runs over, the one named last changes fastest.
Arguments:
- vorticity: float32 [3, 128, 512, 1024], P(None, 'azi', 'ra'), may hold values from -6 to 6
- rotor_field: bfloat16 [3, 128, 512, 1024], P(None, 'azi', 'ra'), may hold values from -6 to 6
- courant: bfloat16 [3, 128, 512, 1024], P(None, 'azi', 'ra'), may hold values from -0.44921875 to 0.44921875
- load_tiles: float32 [16, 32, 128, 384], P('azi', 'ra'), may hold values from -6 to 6
- tile_block: int32 [16, 32, 128], P('azi', 'ra'), may hold values from 0 to 1023
- tile_count: int32 [16, 32, 32], P('azi', 'ra'), may hold values from 0 to 4, as said below
Outputs:
- vorticity_next: float32 [3, 128, 512, 1024], P(None, 'azi', 'ra')
Inputs may be any that keep to these rules, and one draw needn't show every extreme that they name: `tile_count`: in every azimuth group of devices one destination radial device receives 4 used slots from every source device; slots at or beyond the count are padding. `tile_block`: several tiles may name the same cell block.
All inputs are finite; a program needn't handle non-finite values.
Results may differ from a plain program's by a relative error of at most 0.0003.
Values may be sent and summed in bfloat16 or wider, within the bound.
A program may use at most 64 MiB of HBM per device.

v0:
```python
import jax
import jax.numpy as jnp
from jax import lax
from jax.sharding import PartitionSpec as P

TS = 128


DIFFUSION = 0.15


def shifted(block, axis, distance):
    devices = range(lax.axis_size(axis))
    route = [((i - distance) % len(devices), i) for i in devices]
    return lax.ppermute(block, axis, route)


def with_halo(block, sides, width, periodic):
    for axis, dim in sides:
        count = lax.axis_size(axis)
        forward = [(i, i + 1) for i in range(count - 1)]
        if periodic:
            forward.append((count - 1, 0))
        backward = [(target, source) for source, target in forward]
        low = lax.ppermute(
            lax.slice_in_dim(block, block.shape[dim] - width, None, axis=dim), axis, forward
        )
        high = lax.ppermute(lax.slice_in_dim(block, 0, width, axis=dim), axis, backward)
        block = jnp.concatenate([low, block, high], axis=dim)
    return block


def advance_cells(
    combined, next_az, prev_az, next_rad, prev_rad, next_ax, prev_ax, courant, inverse, source_term
):
    velocity = courant.astype(jnp.float32)
    inverse_sq = inverse * inverse
    up_rad = next_rad - combined
    down_rad = combined - prev_rad
    up_az = next_az - combined
    down_az = combined - prev_az
    up_ax = next_ax - combined
    down_ax = combined - prev_ax
    laplace = up_rad - down_rad + 0.25 * inverse * (up_rad + down_rad)
    laplace = laplace + inverse_sq * (up_az - down_az) + (up_ax - down_ax)
    advect = 0.5 * (
        velocity[0] * (up_rad + down_rad)
        + velocity[1] * inverse * (up_az + down_az)
        + velocity[2] * (up_ax + down_ax)
    )
    coupling_rad = -0.25 * inverse_sq * combined[0] - 0.5 * inverse_sq * (next_az[1] - prev_az[1])
    coupling_az = -0.25 * inverse_sq * combined[1] + 0.5 * inverse_sq * (next_az[0] - prev_az[0])
    coupling = jnp.stack([coupling_rad, coupling_az, jnp.zeros_like(combined[2])])
    increment = DIFFUSION * (laplace + coupling) - advect + source_term
    return combined + increment


def body(vorticity, rotor_field, courant, load_tiles, tile_block, tile_count):
    cells_az = vorticity.shape[1]
    cells_rad = vorticity.shape[2]
    cells_ax = vorticity.shape[3]
    n_radial = lax.axis_size("ra")
    radial_pos = lax.axis_index("ra")
    row_index = (radial_pos * cells_rad + lax.iota(jnp.int32, cells_rad)).astype(jnp.float32)
    radius = 0.5 + (row_index + 0.5) / (cells_rad * n_radial)
    inverse = (1.0 / radius)[:, None]
    capacity = load_tiles.shape[2] // n_radial
    tile_vals = load_tiles.reshape(n_radial, capacity, load_tiles.shape[3])
    count_vec = tile_count.reshape(n_radial)
    live_mask = (
        lax.broadcasted_iota(jnp.int32, (n_radial, capacity), 1) < count_vec[:, None]
    ).astype(jnp.float32)
    tile_vals = tile_vals * live_mask[:, :, None]
    block_ids = tile_block.reshape(n_radial, capacity)
    recv_vals, recv_ids = (
        lax.all_to_all(tile_vals, "ra", split_axis=0, concat_axis=0, tiled=True),
        lax.all_to_all(block_ids, "ra", split_axis=0, concat_axis=0, tiled=True),
    )
    arranged = recv_vals.reshape(-1, 3, TS).transpose(1, 0, 2)
    block_total = cells_az * cells_rad * (cells_ax // TS)
    source_term = (
        jnp.zeros((3, block_total, TS), jnp.float32).at[:, recv_ids.reshape(-1)].add(arranged)
    )
    source_term = source_term.reshape(3, cells_az, cells_rad, cells_ax)
    turned = shifted(rotor_field, "azi", 1)
    combined = vorticity + turned.astype(jnp.float32)
    sector_ext = with_halo(combined, (("azi", 1),), 1, True)
    radial_ext = with_halo(combined, (("ra", 2),), 1, False)
    pad_ax = jnp.pad(combined, ((0, 0), (0, 0), (0, 0), (1, 1)))
    return advance_cells(
        combined,
        sector_ext[:, 2:],
        sector_ext[:, :-2],
        radial_ext[:, :, 2:],
        radial_ext[:, :, :-2],
        pad_ax[:, :, :, 2:],
        pad_ax[:, :, :, :-2],
        courant,
        inverse,
        source_term,
    )


def solution(mesh):
    in_specs = (
        P(None, "azi", "ra", None),
        P(None, "azi", "ra", None),
        P(None, "azi", "ra", None),
        P("azi", "ra", None, None),
        P("azi", "ra", None),
        P("azi", "ra", None),
    )
    out_specs = P(None, "azi", "ra", None)
    return jax.shard_map(body, mesh=mesh, in_specs=in_specs, out_specs=out_specs, check_vma=False)
```

profile of v0, /device:TPU:22, one launch (start us, length us, event | category | flops | bytes accessed | tf_op | source)
XLA Modules:
  0.0 98.6 jit_solution(4213470067449764194)
XLA Ops:
  0.0 5.6 %collective-permute-start = (bf16[3,8,16,1024]{3,2,1,0:T(8,128)(2,1)}, bf16[3,8,16,1024]{3,2,1,0:T(8,128)(2,1)}, u32[]{:S(2)}, u32[]{:S(2)}) collective-permute-start(bf16[3,8,16,1024]{3,2,1,0:T(8,128)(2,1)} %param.7), channel_id=1, source_target_pairs={{480,0},{0,32},{32,64},{64,96},{96,128},{128,160},{160,192},{192,2... | collective-permute-start | bytes 2359304 | tf_op jit(solution)/shard_map/ppermute | solution.py:15
  5.6 0.6 broadcast.215
  6.2 1.3 %reduce.6 = s32[128]{0:T(128)S(1)} reduce(s32[1,1,128]{2,1,0:T(1,128)} %param.10, s32[]{:T(128)} %broadcast.215), dimensions={0,1}, to_apply=%param.10.reduce_sub_computation.3 | reduce | bytes 1028 | tf_op args[4]
  7.5 0.7 all_to_all.9
  8.2 10.8 %all-to-all-start = ((s32[32,1,4]{2,1,0:T(1,128)}), s32[32,1,4]{2,1,0:T(1,128)S(1)}, u32[]{:S(2)}, u32[]{:S(2)}) async-start(s32[32,1,4]{2,1,0:T(1,128)} %bitcast.3), calls=%async_computation | async-start | bytes 32768 | tf_op jit(solution)/shard_map/all_to_all | solution.py:77
  19.0 1.3 %convert_element_type.41 = f32[3,8,16,1024]{3,2,1,0:T(8,128)S(1)} convert(bf16[3,8,16,1024]{3,2,1,0:T(8,128)(2,1)} %param.8) | non-fusion elementwise | flops 393216 | bytes 2359296 | tf_op jit(solution)/shard_map/convert_element_type | solution.py:36
  20.3 0.0 copy-start.2
  20.4 0.9 slice_bitcast_fusion.1
  21.3 0.1 fusion.21
  21.4 0.1 reshape.106
  21.4 0.8 broadcast_multiply_fusion
  22.2 17.4 %all-to-all-done = s32[32,1,4]{2,1,0:T(1,128)S(1)} async-done(((s32[32,1,4]{2,1,0:T(1,128)}), s32[32,1,4]{2,1,0:T(1,128)S(1)}, u32[]{:S(2)}, u32[]{:S(2)}) %all-to-all-start) | async-done | bytes 544 | tf_op jit(solution)/shard_map/all_to_all | solution.py:77
  39.7 15.3 %all-to-all-start.1 = ((f32[32,4,384]{2,1,0:T(4,128)}), f32[32,4,384]{2,1,0:T(4,128)S(1)}, u32[]{:S(2)}, u32[]{:S(2)}) async-start(f32[32,4,384]{2,1,0:T(4,128)} %broadcast_multiply_fusion), calls=%async_computation.1 | async-start | bytes 393216 | tf_op jit(solution)/shard_map/all_to_all | solution.py:76
  54.9 0.1 pad.7.clone
  55.0 0.7 reduce.7
  55.7 0.1 reshape.105
  55.8 9.0 %all-to-all-done.1 = f32[32,4,384]{2,1,0:T(4,128)S(1)} async-done(((f32[32,4,384]{2,1,0:T(4,128)}), f32[32,4,384]{2,1,0:T(4,128)S(1)}, u32[]{:S(2)}, u32[]{:S(2)}) %all-to-all-start.1) | async-done | bytes 196640 | tf_op jit(solution)/shard_map/all_to_all | solution.py:76
  64.8 0.1 reshape.107
  64.9 0.3 broadcast_in_dim.2
  65.2 4.9 %scatter_fusion = f32[3,1024,128]{2,0,1:T(4,128)S(1)} fusion(f32[3,1024,128]{2,0,1:T(4,128)S(1)} %broadcast_in_dim.2, s32[128]{0:T(128)S(1)} %fusion.22, f32[128,3,128]{2,1,0:T(4,128)S(1)} %reshape.107), kind=kCustom, calls=%fused_computation | custom fusion | flops 49152 | bytes 590336 | tf_op jit(solution)/shard_map/scatter-add | solution.py:82
  70.1 1.2 %copy.9 = f32[3,1024,128]{2,1,0:T(8,128)} copy(f32[3,1024,128]{2,0,1:T(4,128)S(1)} %scatter_fusion) | data formatting | bytes 3145728 | tf_op jit(solution)/shard_map/scatter-add | solution.py:82
  71.4 1.5 %reshape.108 = f32[3,8,16,1024]{3,2,1,0:T(8,128)S(1)} reshape(f32[3,1024,128]{2,1,0:T(8,128)} %copy.9) | data formatting | bytes 3145728 | tf_op jit(solution)/shard_map/reshape | solution.py:84
  72.9 1.8 %convert_add_fusion = f32[3,8,16,1024]{3,2,1,0:T(8,128)S(1)} fusion(f32[3,8,16,1024]{3,2,1,0:T(8,128)} %param.6, bf16[3,8,16,1024]{3,2,1,0:T(8,128)(2,1)} %collective-permute-done), kind=kLoop, calls=%fused_computation.26 | loop fusion | flops 786432 | bytes 3932160 | tf_op jit(solution)/shard_map/add | solution.py:86
  74.8 1.9 %collective-permute-start.4 = (f32[3,1,16,1024]{3,2,1,0:T(8,128)S(1)}, f32[3,1,16,1024]{3,2,1,0:T(8,128)S(1)}, u32[]{:S(2)}, u32[]{:S(2)}) collective-permute-start(f32[3,1,16,1024]{3,2,1,0:T(8,128)S(1)} %get-tuple-element.13), channel_id=1, source_target_pairs={{0,32},{32,64},{64,96},{96,128},{128,160},{160,192},{192,224},{224... | collective-permute-start | bytes 589832 | tf_op jit(solution)/shard_map/ppermute | solution.py:25
  76.7 3.9 %collective-permute-start.3 = (f32[3,1,16,1024]{3,2,1,0:T(8,128)S(1)}, f32[3,1,16,1024]{3,2,1,0:T(8,128)S(1)}, u32[]{:S(2)}, u32[]{:S(2)}) collective-permute-start(f32[3,1,16,1024]{3,2,1,0:T(8,128)S(1)} %get-tuple-element.12), channel_id=1, source_target_pairs={{32,0},{64,32},{96,64},{128,96},{160,128},{192,160},{224,192},{256... | collective-permute-start | bytes 589832 | tf_op jit(solution)/shard_map/ppermute | solution.py:28
  80.6 0.2 fusion.24
  80.8 1.3 %collective-permute-start.1 = (f32[3,8,1,1024]{3,2,1,0:T(1,128)S(1)}, f32[3,8,1,1024]{3,2,1,0:T(1,128)S(1)}, u32[]{:S(2)}, u32[]{:S(2)}) collective-permute-start(f32[3,8,1,1024]{3,2,1,0:T(1,128)S(1)} %get-tuple-element.11), channel_id=1, source_target_pairs={{1,0},{2,1},{3,2},{4,3},{5,4},{6,5},{7,6},{8,7},{9,8},{10,9},{11,1... | collective-permute-start | bytes 294920 | tf_op jit(solution)/shard_map/ppermute | solution.py:28
  82.1 3.0 %collective-permute-start.2 = (f32[3,8,1,1024]{3,2,1,0:T(1,128)S(1)}, f32[3,8,1,1024]{3,2,1,0:T(1,128)S(1)}, u32[]{:S(2)}, u32[]{:S(2)}) collective-permute-start(f32[3,8,1,1024]{3,2,1,0:T(1,128)S(1)} %get-tuple-element.10), channel_id=1, source_target_pairs={{0,1},{1,2},{2,3},{3,4},{4,5},{5,6},{6,7},{7,8},{8,9},{9,10},{10,1... | collective-permute-start | bytes 294920 | tf_op jit(solution)/shard_map/ppermute | solution.py:25
  85.1 9.1 %collective-permute-done.3 = f32[3,1,16,1024]{3,2,1,0:T(8,128)S(1)} collective-permute-done((f32[3,1,16,1024]{3,2,1,0:T(8,128)S(1)}, f32[3,1,16,1024]{3,2,1,0:T(8,128)S(1)}, u32[]{:S(2)}, u32[]{:S(2)}) %collective-permute-start.3) | collective-permute-done | bytes 196640 | tf_op jit(solution)/shard_map/ppermute | solution.py:28
  94.2 0.2 fusion.15
  94.5 0.8 copy-done
  95.3 3.3 %fusion.11 = f32[3,8,16,1024]{3,2,1,0:T(8,128)} fusion(f32[3,8,16,1024]{3,2,1,0:T(8,128)S(1)} %convert_add_fusion, f32[3,8,16,1024]{3,2,1,0:T(8,128)S(1)} %reshape.108, f32[1,8,16,1024]{3,2,1,0:T(8,128)S(1)} %get-tuple-element.6, f32[1,8,16,1024]{3,2,1,0:T(8,128)S(1)} %get-tuple-element.5, f32[3,1,16,1024]{3,2,1,0:T(8,128)S(1)} %collective-permute-done.3, ...), kind=kLoop, calls=%fused_computation.25 | loop fusion | flops 13369344 | bytes 7929996 | tf_op jit(solution)/shard_map/add | solution.py:55
  (13 shorter events, 0.1 us)
Async XLA Ops:
  0.0 72.9 %collective-permute-start = (bf16[3,8,16,1024]{3,2,1,0:T(8,128)(2,1)}, bf16[3,8,16,1024]{3,2,1,0:T(8,128)(2,1)}, u32[]{:S(2)}, u32[]{:S(2)}) collective-permute-start(bf16[3,8,16,1024]{3,2,1,0:T(8,128)(2,1)} %param.7), channel_id=1, source_target_pairs={{480,0},{0,32},{32,64},{64,96},{96,128},{128,160},{160,192},{192,2... | collective-permute-start | bytes 2359304 | tf_op jit(solution)/shard_map/ppermute | solution.py:15
  8.2 31.5 %all-to-all-start = ((s32[32,1,4]{2,1,0:T(1,128)}), s32[32,1,4]{2,1,0:T(1,128)S(1)}, u32[]{:S(2)}, u32[]{:S(2)}) async-start(s32[32,1,4]{2,1,0:T(1,128)} %bitcast.3), calls=%async_computation | async-start | bytes 32768 | tf_op jit(solution)/shard_map/all_to_all | solution.py:77
  20.3 1.0 copy-start.2
  20.4 1.0 %copy-start.1 = (f32[1,1,128,384]{3,2,1,0:T(8,128)S(1)}, f32[1,1,128,384]{3,2,1,0:T(8,128)}, u32[]{:S(2)}) copy-start(f32[1,1,128,384]{3,2,1,0:T(8,128)} %param.9) | copy-start | bytes 589828
  39.7 25.1 %all-to-all-start.1 = ((f32[32,4,384]{2,1,0:T(4,128)}), f32[32,4,384]{2,1,0:T(4,128)S(1)}, u32[]{:S(2)}, u32[]{:S(2)}) async-start(f32[32,4,384]{2,1,0:T(4,128)} %broadcast_multiply_fusion), calls=%async_computation.1 | async-start | bytes 393216 | tf_op jit(solution)/shard_map/all_to_all | solution.py:76
  74.8 10.4 %collective-permute-start.4 = (f32[3,1,16,1024]{3,2,1,0:T(8,128)S(1)}, f32[3,1,16,1024]{3,2,1,0:T(8,128)S(1)}, u32[]{:S(2)}, u32[]{:S(2)}) collective-permute-start(f32[3,1,16,1024]{3,2,1,0:T(8,128)S(1)} %get-tuple-element.13), channel_id=1, source_target_pairs={{0,32},{32,64},{64,96},{96,128},{128,160},{160,192},{192,224},{224... | collective-permute-start | bytes 589832 | tf_op jit(solution)/shard_map/ppermute | solution.py:25
  76.7 17.6 %collective-permute-start.3 = (f32[3,1,16,1024]{3,2,1,0:T(8,128)S(1)}, f32[3,1,16,1024]{3,2,1,0:T(8,128)S(1)}, u32[]{:S(2)}, u32[]{:S(2)}) collective-permute-start(f32[3,1,16,1024]{3,2,1,0:T(8,128)S(1)} %get-tuple-element.12), channel_id=1, source_target_pairs={{32,0},{64,32},{96,64},{128,96},{160,128},{192,160},{224,192},{256... | collective-permute-start | bytes 589832 | tf_op jit(solution)/shard_map/ppermute | solution.py:28
  80.8 13.7 %collective-permute-start.1 = (f32[3,8,1,1024]{3,2,1,0:T(1,128)S(1)}, f32[3,8,1,1024]{3,2,1,0:T(1,128)S(1)}, u32[]{:S(2)}, u32[]{:S(2)}) collective-permute-start(f32[3,8,1,1024]{3,2,1,0:T(1,128)S(1)} %get-tuple-element.11), channel_id=1, source_target_pairs={{1,0},{2,1},{3,2},{4,3},{5,4},{6,5},{7,6},{8,7},{9,8},{10,9},{11,1... | collective-permute-start | bytes 294920 | tf_op jit(solution)/shard_map/ppermute | solution.py:28
  82.1 12.4 %collective-permute-start.2 = (f32[3,8,1,1024]{3,2,1,0:T(1,128)S(1)}, f32[3,8,1,1024]{3,2,1,0:T(1,128)S(1)}, u32[]{:S(2)}, u32[]{:S(2)}) collective-permute-start(f32[3,8,1,1024]{3,2,1,0:T(1,128)S(1)} %get-tuple-element.10), channel_id=1, source_target_pairs={{0,1},{1,2},{2,3},{3,4},{4,5},{5,6},{6,7},{7,8},{8,9},{9,10},{10,1... | collective-permute-start | bytes 294920 | tf_op jit(solution)/shard_map/ppermute | solution.py:25
  94.2 1.0 %copy-start = (f32[8,16,1024]{2,1,0:T(8,128)S(1)}, f32[8,16,1024]{2,1,0:T(8,128)}, u32[]{:S(2)}) copy-start(f32[8,16,1024]{2,1,0:T(8,128)} %get-tuple-element.9) | copy-start | bytes 1572868
where the time goes:
time: 99.1 us; the launch traced here: 98.6 us
  starting transfers between devices  41.9 us (42%)
  waiting for transfers between devices  35.5 us (36%)
  other arithmetic  15.4 us (16%)
  local copies, waits for them, and re-layouts  5.62 us (6%)
    all_to_all x1, waiting for transfers between devices, body(): lax.all_to_all(block_ids, 'ra', split_axis=0, concat_axis=0, tiled=True)  17.4 us
    all_to_all x1, starting transfers between devices, body(): lax.all_to_all(tile_vals, 'ra', split_axis=0, concat_axis=0, tiled=True)  15.3 us
    all_to_all x1, starting transfers between devices, body(): lax.all_to_all(block_ids, 'ra', split_axis=0, concat_axis=0, tiled=True)  10.8 us
    ppermute x2, waiting for transfers between devices, with_halo(): lax.ppermute(lax.slice_in_dim(block, 0, width, axis=dim), axis, backward)  9.12 us
    all_to_all x1, waiting for transfers between devices, body(): lax.all_to_all(tile_vals, 'ra', split_axis=0, concat_axis=0, tiled=True)  8.97 us
    ppermute x1, starting transfers between devices, shifted(): return lax.ppermute(block, axis, route)  5.61 us
    ppermute x2, starting transfers between devices, with_halo(): lax.ppermute(lax.slice_in_dim(block, 0, width, axis=dim), axis, backward)  5.21 us
    ppermute x2, starting transfers between devices, with_halo(): lax.ppermute(lax.slice_in_dim(block, block.shape[dim] - width, None, axis...  4.96 us
  transfers between devices with their start and end apart: 7, of which 3 were waited for; matrix products, arithmetic and copies ran while one was open for 15% of the time, Pallas kernels for 0%

commit v1 on v0

v1 whole, which is shorter than its diff:
```python
import functools

import jax
import jax.numpy as jnp
from jax import lax
from jax.experimental import pallas as pl
from jax.experimental.pallas import tpu as pltpu
from jax.sharding import PartitionSpec as P

TS = 128
DIFFUSION = 0.15
MESH = pl.DeviceIdType.MESH
CHIP_X = 4

AROUND = (3, 4)
THROUGH = (0, 1, 2, 6)
STRAIGHT = (7, 0, 1, 2, 6, 5)
ORDER = (7, 0, 1, 2, 3, 4, 6, 5)


def kernel(
    vort, rotor, cour, tiles, tile_id, tile_n, out,
    vbuf, cbuf, rin, own0, comb, obuf, src, vup,
    relay_a, relay_b, relay_p, edge_out, edge_in,
    tbuf, idbuf, cntbuf, sbuf, trecv, tsib, tmat,
    lsem, osem, r_send, r_recv, a_send, a_recv, b_send, b_recv, c_send,
    p_send, p_recv, q_send, h_send, h_recv, e_send, e_recv, t_send, t_recv,
):
    n_azi, n_ra = lax.axis_size("azi"), lax.axis_size("ra")
    n_y = n_azi // CHIP_X
    n_chip = n_ra // 2
    rows_az, rows_rad, cells_ax = vbuf.shape[1:]
    j, r = lax.axis_index("azi"), lax.axis_index("ra")
    x, y = j % CHIP_X, j // CHIP_X
    chip, core = r // 2, r % 2
    first, last = x == 0, x == CHIP_X - 1

    def at(xx, yy):
        return ((yy % n_y) * CHIP_X + xx % CHIP_X, r)

    following = ((j + 1) % n_azi, r)
    preceding = ((j + n_azi - 1) % n_azi, r)
    up_x, down_x = at(x + 1, y), at(x + 3, y)
    up_y, down_y = at(x, y + 1), at(x, y + n_y - 1)
    sibling = (j, chip * 2 + 1 - core)

    def local(ref, dst, k):
        return pltpu.make_async_copy(ref, dst, lsem.at[k])

    def row(ref, k):
        return ref.at[:, pl.ds(k, 1)]

    loads = [
        local(tiles.at[0, 0], tbuf, 0),
        local(tile_id.at[0], idbuf, 1),
        local(tile_n.at[0], cntbuf, 2),
        local(vort, vbuf, 3),
        local(row(rotor, 0), own0, 4),
        local(cour, cbuf, 5),
    ]
    for load in loads:
        load.start()

    bar = pltpu.get_barrier_semaphore()

    def greet(device):
        pl.semaphore_signal(bar, inc=1, device_id=device, device_id_type=MESH)

    greet(following)
    greet(preceding)
    greet(sibling)
    for d in range(1, n_chip):
        greet((j, ((chip + d) % n_chip) * 2 + core))
    pl.when(last)(lambda: greet(up_x))
    pl.when(first)(lambda: greet(down_x))
    pl.when(x == 2)(lambda: greet(at(1, y + 1)))
    pl.when(x == 1)(lambda: greet(at(2, y + n_y - 1)))

    @pl.when(first)
    def _():
        greet(up_y)
        greet(down_y)

    outer_low = jnp.logical_and(core == 0, r > 0)
    outer_high = jnp.logical_and(core == 1, r < n_ra - 1)
    pl.when(outer_low)(lambda: greet((j, r - 1)))
    pl.when(outer_high)(lambda: greet((j, r + 1)))

    loads[0].wait()
    loads[1].wait()
    loads[2].wait()
    slots = tbuf.shape[0]
    slot = lax.broadcasted_iota(jnp.int32, (slots, slots), 0)
    lane = lax.broadcasted_iota(jnp.int32, (slots, slots), 1)
    ids = jnp.broadcast_to(idbuf[...].astype(jnp.float32), (slots, slots))
    id_col = jnp.sum(jnp.where(slot == lane, ids, 0.0), axis=1, keepdims=True)
    capacity = slots // n_ra
    slot_n = lax.broadcasted_iota(jnp.int32, (slots, n_ra), 0)
    lane_n = lax.broadcasted_iota(jnp.int32, (slots, n_ra), 1)
    counts = jnp.broadcast_to(cntbuf[...].astype(jnp.float32), (slots, n_ra))
    count_col = jnp.sum(
        jnp.where(slot_n // capacity == lane_n, counts, 0.0), axis=1, keepdims=True
    )
    used = (slot % capacity).astype(jnp.float32) < count_col
    width = tbuf.shape[1]
    sbuf[:, :width] = tbuf[...]
    sbuf[:, width:] = jnp.where(used, id_col, -1.0)
    group = 2 * capacity
    trecv[pl.ds(chip, 1)] = sbuf[pl.ds(pl.multiple_of(chip * group, group), group)][None]

    others = 3 + (n_chip - 1) + 1 + 2 * first.astype(jnp.int32)
    others = others + outer_low.astype(jnp.int32) + outer_high.astype(jnp.int32)
    pl.semaphore_wait(bar, others)

    def remote(source, target, send, recv, device):
        return pltpu.make_async_remote_copy(
            src_ref=source, dst_ref=target, send_sem=send, recv_sem=recv,
            device_id=device, device_id_type=MESH,
        )

    def straight(k):
        return remote(row(rotor, k), row(rin, k), r_send.at[k], r_recv.at[k], following)

    def through(k):
        i = THROUGH.index(k)
        return remote(row(rotor, k), row(relay_p, i), r_send.at[k], p_recv.at[i], up_x)

    def through_on(k):
        i = THROUGH.index(k)
        return remote(row(relay_p, i), row(rin, k), q_send.at[i], r_recv.at[k], up_y)

    def around(k):
        i = AROUND.index(k)
        return remote(row(rotor, k), row(relay_a, i), a_send.at[i], a_recv.at[i], down_x)

    def around_on(k, device):
        i = AROUND.index(k)
        return remote(row(relay_a, i), row(relay_b, i), b_send.at[i], b_recv.at[i], device)

    def around_end(k):
        i = AROUND.index(k)
        return remote(row(relay_b, i), row(rin, k), c_send.at[i], r_recv.at[k], down_x)

    low_edge = remote(row(vort, 0), vup, h_send.at[0], h_recv.at[0], preceding)
    high_edge = remote(row(comb, rows_az), row(comb, 0), h_send.at[1], h_recv.at[1], following)

    def radial(k, side, device):
        return remote(
            edge_out.at[side, k], edge_in.at[side, k], e_send.at[side, k], e_recv.at[side, k], device
        )

    def tile_copy(d):
        to = (chip + d) % n_chip
        return remote(
            sbuf.at[pl.ds(pl.multiple_of(to * group, group), group)], trecv.at[chip],
            t_send.at[d], t_recv.at[d], (j, to * 2 + core),
        )

    exchange = remote(trecv, tsib, t_send.at[0], t_recv.at[0], sibling)
    has_low, has_high = r > 0, r < n_ra - 1

    def start_row(k):
        if k in THROUGH:
            pl.when(last)(lambda: through(k).start())
            pl.when(jnp.logical_not(last))(lambda: straight(k).start())
        else:
            straight(k).start()

    start_row(7)
    around(AROUND[0]).start()
    low_edge.start()
    start_row(0)
    around(AROUND[1]).start()
    for d in range(1, n_chip):
        tile_copy(d).start()
    for k in STRAIGHT[2:]:
        start_row(k)

    @pl.when(jnp.logical_not(has_low))
    def _():
        edge_in[0] = jnp.zeros_like(edge_in[0])

    @pl.when(jnp.logical_not(has_high))
    def _():
        edge_in[1] = jnp.zeros_like(edge_in[1])

    def take(k):
        straight(k).wait_recv()
        for c in range(3):
            value = vbuf[c, k] + rin[c, k].astype(jnp.float32)
            comb[c, k + 1] = value
            edge_out[0, k, c : c + 1] = value[rows_rad - 1 :]
            edge_out[1, k, c : c + 1] = value[:1]
        pl.when(has_high)(lambda: radial(k, 0, (j, r + 1)).start())
        pl.when(has_low)(lambda: radial(k, 1, (j, r - 1)).start())

    def relay_through(k):
        @pl.when(first)
        def _():
            through(k).wait_recv()
            through_on(k).start()

    def relay_first(k):
        around(k).wait_recv()
        pl.when(x == 2)(lambda: around_on(k, at(1, y + 1)).start())
        pl.when(x != 2)(lambda: around_on(k, down_x).start())

    def relay_second(k):
        around_on(k, down_x).wait_recv()
        around_end(k).start()

    axial = lax.broadcasted_iota(jnp.int32, (rows_rad, cells_ax), 1)
    radial_row = lax.broadcasted_iota(jnp.int32, (rows_rad, cells_ax), 0)
    position = (r * rows_rad + radial_row).astype(jnp.float32)
    inverse = 1.0 / (0.5 + (position + 0.5) / (rows_rad * n_ra))
    inverse_sq = inverse * inverse

    def stencil(k):
        v0 = cbuf[0, k].astype(jnp.float32)
        v1 = cbuf[1, k].astype(jnp.float32)
        v2 = cbuf[2, k].astype(jnp.float32)
        rad = (0.25 * DIFFUSION) * inverse - 0.5 * v0
        azi_even = DIFFUSION * inverse_sq
        azi_odd = 0.5 * v1 * inverse
        axi = 0.5 * v2
        middle = (1.0 - 4.0 * DIFFUSION) - (2.0 * DIFFUSION) * inverse_sq
        turn = (0.5 * DIFFUSION) * inverse_sq
        for c in range(3):
            f = comb[c, k + 1]
            nxt, prv = comb[c, k + 2], comb[c, k]
            up = pltpu.roll(f, rows_rad - 1, 0)
            up = jnp.where(radial_row == rows_rad - 1, edge_in[1, k, c : c + 1], up)
            down = pltpu.roll(f, 1, 0)
            down = jnp.where(radial_row == 0, edge_in[0, k, c : c + 1], down)
            right = jnp.where(axial == cells_ax - 1, 0.0, pltpu.roll(f, cells_ax - 1, 1))
            left = jnp.where(axial == 0, 0.0, pltpu.roll(f, 1, 1))
            total = middle * f + src[c, k]
            total = total + DIFFUSION * ((up + down) + (right + left))
            total = total + rad * (up - down) - axi * (right - left)
            total = total + azi_even * (nxt + prv) - azi_odd * (nxt - prv)
            if c == 0:
                total = total - (0.5 * turn) * f - turn * (comb[1, k + 2] - comb[1, k])
            elif c == 1:
                total = total - (0.5 * turn) * f + turn * (comb[0, k + 2] - comb[0, k])
            obuf[c, k] = total

    def finish(k):
        pl.when(has_low)(lambda: radial(k, 0, (j, r)).wait_recv())
        pl.when(has_high)(lambda: radial(k, 1, (j, r)).wait_recv())
        stencil(k)
        pltpu.make_async_copy(row(obuf, k), row(out, k), osem.at[k]).start()

    loads[3].wait()
    take(7)
    high_edge.start()
    relay_first(AROUND[0])
    relay_through(0)
    take(0)
    relay_first(AROUND[1])
    relay_through(1)
    for d in range(1, n_chip):
        tile_copy(d).wait_recv()
    exchange.start()
    relay_second(AROUND[0])
    take(1)
    relay_through(2)
    relay_second(AROUND[1])

    exchange.wait_recv()
    keep = (slot % group) // capacity == core
    halves = []
    for i, got in enumerate((trecv, tsib)):
        part = got[...].reshape(slots, width + slots)
        value = part[:, :width]
        top = value.astype(jnp.bfloat16)
        tmat[i * slots : (i + 1) * slots] = top
        tmat[(2 + i) * slots : (3 + i) * slots] = (value - top.astype(jnp.float32)).astype(
            jnp.bfloat16
        )
        halves.append(jnp.where(keep, part[:, width:], -1.0).T)
    blocks = jnp.concatenate(halves, axis=1)
    m = lax.broadcasted_iota(jnp.int32, blocks.shape, 0)
    per_row = cells_ax // TS
    local_block = (m % rows_rad) * per_row + m // rows_rad
    for a in range(rows_az):
        wanted = (local_block + a * rows_rad * per_row).astype(jnp.float32)
        hot = jnp.where(blocks == wanted, 1.0, 0.0).astype(jnp.bfloat16)
        placed = jnp.dot(
            jnp.concatenate([hot, hot], axis=1), tmat[...], preferred_element_type=jnp.float32
        )
        for b in range(per_row):
            for c in range(3):
                src[c, a, :, b * TS : (b + 1) * TS] = placed[
                    b * rows_rad : (b + 1) * rows_rad, c * TS : (c + 1) * TS
                ]

    loads[4].wait()
    loads[5].wait()
    low_edge.wait_recv()
    for c in range(3):
        comb[c, rows_az + 1] = vup[c, 0] + own0[c, 0].astype(jnp.float32)
    high_edge.wait_recv()
    finish(0)
    relay_through(6)
    take(2)
    finish(1)
    take(3)
    finish(2)
    take(4)
    finish(3)
    take(6)
    finish(7)
    take(5)
    finish(4)
    finish(6)
    finish(5)

    for k in STRAIGHT:
        straight(k).wait_send()
    for k in AROUND:
        around(k).wait_send()
        around_on(k, down_x).wait_send()
        around_end(k).wait_send()

    @pl.when(first)
    def _():
        for k in THROUGH:
            through_on(k).wait_send()

    low_edge.wait_send()
    high_edge.wait_send()
    for d in range(1, n_chip):
        tile_copy(d).wait_send()
    exchange.wait_send()
    for k in range(rows_az):
        pl.when(has_high)(lambda k=k: radial(k, 0, (j, r)).wait_send())
        pl.when(has_low)(lambda k=k: radial(k, 1, (j, r)).wait_send())
        pltpu.make_async_copy(row(obuf, k), row(out, k), osem.at[k]).wait()


def body(vorticity, rotor_field, courant, load_tiles, tile_block, tile_count):
    shape = vorticity.shape
    _, rows_az, rows_rad, cells_ax = shape
    slots, width = load_tiles.shape[2:]
    n_ra = lax.axis_size("ra")
    n_chip = n_ra // 2
    group = slots // n_chip
    one_row = (3, 1, rows_rad, cells_ax)

    def relay(n):
        return pltpu.VMEM((3, n, rows_rad, cells_ax), jnp.bfloat16)

    dma = pltpu.SemaphoreType.DMA
    around, through = len(AROUND), len(THROUGH)
    scratch = [
        pltpu.VMEM(shape, jnp.float32),
        pltpu.VMEM(shape, jnp.bfloat16),
        pltpu.VMEM(shape, jnp.bfloat16),
        pltpu.VMEM(one_row, jnp.bfloat16),
        pltpu.VMEM((3, rows_az + 2, rows_rad, cells_ax), jnp.float32),
        pltpu.VMEM(shape, jnp.float32),
        pltpu.VMEM(shape, jnp.float32),
        pltpu.VMEM(one_row, jnp.float32),
        relay(around),
        relay(around),
        relay(through),
        pltpu.VMEM((2, rows_az, 3, cells_ax), jnp.float32),
        pltpu.VMEM((2, rows_az, 3, cells_ax), jnp.float32),
        pltpu.VMEM((slots, width), jnp.float32),
        pltpu.VMEM((1, slots), jnp.int32),
        pltpu.VMEM((1, n_ra), jnp.int32),
        pltpu.VMEM((slots, width + slots), jnp.float32),
        pltpu.VMEM((n_chip, group, width + slots), jnp.float32),
        pltpu.VMEM((n_chip, group, width + slots), jnp.float32),
        pltpu.VMEM((4 * slots, width), jnp.bfloat16),
        dma((6,)),
        dma((rows_az,)),
        dma((rows_az,)),
        dma((rows_az,)),
        dma((around,)),
        dma((around,)),
        dma((around,)),
        dma((around,)),
        dma((around,)),
        dma((through,)),
        dma((through,)),
        dma((through,)),
        dma((2,)),
        dma((2,)),
        dma((2, rows_az)),
        dma((2, rows_az)),
        dma((n_chip,)),
        dma((n_chip,)),
    ]
    return pl.pallas_call(
        kernel,
        name="step",
        out_shape=jax.ShapeDtypeStruct(shape, jnp.float32),
        in_specs=[pl.BlockSpec(memory_space=pltpu.HBM)] * 6,
        out_specs=pl.BlockSpec(memory_space=pl.ANY),
        scratch_shapes=scratch,
        compiler_params=pltpu.CompilerParams(
            collective_id=0, has_side_effects=True, vmem_limit_bytes=40 * 1024 * 1024
        ),
    )(vorticity, rotor_field, courant, load_tiles, tile_block, tile_count)


def solution(mesh):
    in_specs = (
        P(None, "azi", "ra", None),
        P(None, "azi", "ra", None),
        P(None, "azi", "ra", None),
        P("azi", "ra", None, None),
        P("azi", "ra", None),
        P("azi", "ra", None),
    )
    out_specs = P(None, "azi", "ra", None)
    return jax.shard_map(body, mesh=mesh, in_specs=in_specs, out_specs=out_specs, check_vma=False)
```

time: 99.1 us -> 63.8 us (0.64)
  the two profiles are of different devices: /device:TPU:22 before, /device:TPU:24 now
where the time goes in v1:
time: 63.8 us; the launch traced here: 63.5 us
  Pallas kernels  56.4 us (88%)
  local copies, waits for them, and re-layouts  7.05 us (11%)
    pallas_call x1, Pallas kernels, body(): pl.pallas_call(kernel, name='step', out_shape=jax.ShapeDtypeStruct(shape,...  56.4 us
    unnamed x13, local copies, waits for them, and re-layouts  7.05 us

profile of v1, /device:TPU:24, one launch (start us, length us, event | category | flops | bytes accessed | tf_op | source)
XLA Modules:
  0.0 63.5 jit_solution(15096500655745322075)
XLA Ops:
  0.0 0.0 copy-start
  0.0 1.4 %copy-done = f32[3,8,16,1024]{3,2,1,0:T(8,128)S(1)} copy-done((f32[3,8,16,1024]{3,2,1,0:T(8,128)S(1)}, f32[3,8,16,1024]{3,2,1,0:T(8,128)}, u32[]{:S(2)}) %copy-start) | copy-done | bytes 1572888
  1.4 0.0 copy-start.1
  1.4 1.1 %copy-done.1 = bf16[3,8,16,1024]{3,2,1,0:T(8,128)(2,1)S(1)} copy-done((bf16[3,8,16,1024]{3,2,1,0:T(8,128)(2,1)S(1)}, bf16[3,8,16,1024]{3,2,1,0:T(8,128)(2,1)}, u32[]{:S(2)}) %copy-start.1) | copy-done | bytes 786456
  2.5 0.0 copy-start.2
  2.5 1.1 %copy-done.2 = bf16[3,8,16,1024]{3,2,1,0:T(8,128)(2,1)S(1)} copy-done((bf16[3,8,16,1024]{3,2,1,0:T(8,128)(2,1)S(1)}, bf16[3,8,16,1024]{3,2,1,0:T(8,128)(2,1)}, u32[]{:S(2)}) %copy-start.2) | copy-done | bytes 786456
  3.7 0.0 copy-start.3
  3.7 0.9 %copy-done.3 = f32[1,1,128,384]{3,2,1,0:T(8,128)S(1)} copy-done((f32[1,1,128,384]{3,2,1,0:T(8,128)S(1)}, f32[1,1,128,384]{3,2,1,0:T(8,128)}, u32[]{:S(2)}) %copy-start.3) | copy-done | bytes 196632
  4.6 0.0 copy-start.4
  4.6 0.7 %copy-done.4 = s32[1,1,128]{2,1,0:T(1,128)S(1)} copy-done((s32[1,1,128]{2,1,0:T(1,128)S(1)}, s32[1,1,128]{2,1,0:T(1,128)}, u32[]{:S(2)}) %copy-start.4) | copy-done | bytes 536
  5.3 0.0 copy-start.5
  5.3 0.7 %copy-done.5 = s32[1,1,32]{2,1,0:T(1,128)S(1)} copy-done((s32[1,1,32]{2,1,0:T(1,128)S(1)}, s32[1,1,32]{2,1,0:T(1,128)}, u32[]{:S(2)}) %copy-start.5) | copy-done | bytes 152
  5.9 56.4 %step.1 = f32[3,8,16,1024]{3,2,1,0:T(8,128)S(1)} custom-call(f32[3,8,16,1024]{3,2,1,0:T(8,128)S(1)} %copy-done, bf16[3,8,16,1024]{3,2,1,0:T(8,128)(2,1)S(1)} %copy-done.1, bf16[3,8,16,1024]{3,2,1,0:T(8,128)(2,1)S(1)} %copy-done.2, f32[1,1,128,384]{3,2,1,0:T(8,128)S(1)} %copy-done.3, s32[1,1,128]{2,1,0:T(1,128)S(1)} %copy-done.4, s32[1,1,32]{2,1,0:T(1,128)S(1)} %copy-done.5), custom_call_target="tpu_custom_call" | custom-call | tf_op jit(solution)/shard_map/step/pallas_call | solution.py:395
  62.3 1.1 %copy.8 = f32[3,8,16,1024]{3,2,1,0:T(8,128)} copy(f32[3,8,16,1024]{3,2,1,0:T(8,128)S(1)} %step.1) | data formatting | bytes 3145728
Async XLA Ops:
  0.0 1.4 %copy-start = (f32[3,8,16,1024]{3,2,1,0:T(8,128)S(1)}, f32[3,8,16,1024]{3,2,1,0:T(8,128)}, u32[]{:S(2)}) copy-start(f32[3,8,16,1024]{3,2,1,0:T(8,128)} %vort.1) | copy-start | bytes 4718596
  1.4 1.1 %copy-start.1 = (bf16[3,8,16,1024]{3,2,1,0:T(8,128)(2,1)S(1)}, bf16[3,8,16,1024]{3,2,1,0:T(8,128)(2,1)}, u32[]{:S(2)}) copy-start(bf16[3,8,16,1024]{3,2,1,0:T(8,128)(2,1)} %rotor.1) | copy-start | bytes 2359300
  2.5 1.1 %copy-start.2 = (bf16[3,8,16,1024]{3,2,1,0:T(8,128)(2,1)S(1)}, bf16[3,8,16,1024]{3,2,1,0:T(8,128)(2,1)}, u32[]{:S(2)}) copy-start(bf16[3,8,16,1024]{3,2,1,0:T(8,128)(2,1)} %cour.1) | copy-start | bytes 2359300
  3.7 0.9 %copy-start.3 = (f32[1,1,128,384]{3,2,1,0:T(8,128)S(1)}, f32[1,1,128,384]{3,2,1,0:T(8,128)}, u32[]{:S(2)}) copy-start(f32[1,1,128,384]{3,2,1,0:T(8,128)} %tiles.1) | copy-start | bytes 589828
  4.6 0.7 %copy-start.4 = (s32[1,1,128]{2,1,0:T(1,128)S(1)}, s32[1,1,128]{2,1,0:T(1,128)}, u32[]{:S(2)}) copy-start(s32[1,1,128]{2,1,0:T(1,128)} %tile_id.1) | copy-start | bytes 1540
  5.3 0.7 %copy-start.5 = (s32[1,1,32]{2,1,0:T(1,128)S(1)}, s32[1,1,32]{2,1,0:T(1,128)}, u32[]{:S(2)}) copy-start(s32[1,1,32]{2,1,0:T(1,128)} %tile_n.1) | copy-start | bytes 388

commit v2 on v1

v2 whole, which is shorter than its diff:
```python
import functools

import jax
import jax.numpy as jnp
from jax import lax
from jax.experimental import pallas as pl
from jax.experimental.pallas import tpu as pltpu
from jax.sharding import PartitionSpec as P

TS = 128
DIFFUSION = 0.15
MESH = pl.DeviceIdType.MESH
CHIP_X = 4

AROUND = (3, 4)
THROUGH = (0, 1, 2, 6, 5)
STRAIGHT = (7, 0, 1, 2, 6, 5)


def kernel(
    vort, rotor, cour, tiles, tile_id, tile_n, out,
    vbuf, cbuf, rbuf, rin, comb, obuf, src, vup,
    relay_a, relay_b, relay_p, edge_f, edge_s, edge_r, edge_out, edge_in,
    tbuf, idbuf, cntbuf, sbuf, trecv, tsib, tmat,
    lsem, osem, r_send, r_recv, a_send, a_recv, b_send, b_recv, c_send,
    p_recv, q_send, h_send, h_recv, e_send, e_recv, t_send, t_recv, up_sem, down_sem,
):
    n_azi, n_ra = lax.axis_size("azi"), lax.axis_size("ra")
    n_y = n_azi // CHIP_X
    n_chip = n_ra // 2
    n_z = n_chip // 2
    rows_az, rows_rad, cells_ax = vbuf.shape[1:]
    j, r = lax.axis_index("azi"), lax.axis_index("ra")
    x, y = j % CHIP_X, j // CHIP_X
    chip, core = r // 2, r % 2
    z = chip % n_z
    first, last = x == 0, x == CHIP_X - 1
    has_low, has_high = r > 0, r < n_ra - 1
    z_low, z_high = z > 0, z < n_z - 1
    near_low = jnp.logical_and(core == 0, z_low)
    near_high = jnp.logical_and(core == 1, z_high)
    seam_low = jnp.logical_and(jnp.logical_and(core == 0, z == 0), has_low)
    seam_high = jnp.logical_and(jnp.logical_and(core == 1, z == n_z - 1), has_high)

    def at(xx, yy):
        return ((yy % n_y) * CHIP_X + xx % CHIP_X, r)

    following = ((j + 1) % n_azi, r)
    preceding = ((j + n_azi - 1) % n_azi, r)
    up_x, down_x = at(x + 1, y), at(x + 3, y)
    up_y, down_y = at(x, y + 1), at(x, y + n_y - 1)
    sibling = (j, chip * 2 + 1 - core)
    above, below = (j, r + 2), (j, r - 2)
    lower, higher = (j, r - 1), (j, r + 1)

    def local(ref, dst, k):
        return pltpu.make_async_copy(ref, dst, lsem.at[k])

    def row(ref, k):
        return ref.at[:, pl.ds(k, 1)]

    loads = [
        local(rotor, rbuf, 0),
        local(vort, vbuf, 1),
        local(tiles.at[0, 0], tbuf, 2),
        local(tile_id.at[0], idbuf, 3),
        local(tile_n.at[0], cntbuf, 4),
        local(cour, cbuf, 5),
    ]
    for load in loads:
        load.start()

    bar = pltpu.get_barrier_semaphore()

    def greet(device):
        pl.semaphore_signal(bar, inc=1, device_id=device, device_id_type=MESH)

    greet(following)
    greet(preceding)
    greet(sibling)
    greet((j, (r + n_ra // 2) % n_ra))
    pl.when(last)(lambda: greet(up_x))
    pl.when(first)(lambda: greet(down_x))
    pl.when(x == 2)(lambda: greet(at(1, y + 1)))
    pl.when(x == 1)(lambda: greet(at(2, y + n_y - 1)))

    @pl.when(first)
    def _():
        greet(up_y)
        greet(down_y)

    pl.when(z_high)(lambda: greet(above))
    pl.when(z_low)(lambda: greet(below))
    pl.when(near_low)(lambda: greet(lower))
    pl.when(near_high)(lambda: greet(higher))
    others = 5 + 2 * first.astype(jnp.int32)
    for near in (z_high, z_low, near_low, near_high):
        others = others + near.astype(jnp.int32)

    loads[0].wait()
    for c in range(3):
        for k in range(rows_az):
            whole = rbuf[c, k].astype(jnp.float32)
            edge_f[c, k : k + 1] = whole[:1]
            edge_f[c, rows_az + k : rows_az + k + 1] = whole[rows_rad - 1 :]
    edge_s[...] = edge_f[...].astype(jnp.bfloat16)

    pl.semaphore_wait(bar, others)

    def remote(source, target, send, recv, device):
        return pltpu.make_async_remote_copy(
            src_ref=source, dst_ref=target, send_sem=send, recv_sem=recv,
            device_id=device, device_id_type=MESH,
        )

    def straight(k):
        return remote(row(rotor, k), row(rin, k), r_send.at[k], r_recv.at[k], following)

    def through(k):
        i = THROUGH.index(k)
        return remote(row(rotor, k), row(relay_p, i), r_send.at[k], p_recv.at[i], up_x)

    def through_on(k):
        i = THROUGH.index(k)
        return remote(row(relay_p, i), row(rin, k), q_send.at[i], r_recv.at[k], up_y)

    def around(k):
        i = AROUND.index(k)
        return remote(row(rotor, k), row(relay_a, i), a_send.at[i], a_recv.at[i], down_x)

    def around_on(k, device):
        i = AROUND.index(k)
        return remote(row(relay_a, i), row(relay_b, i), b_send.at[i], b_recv.at[i], device)

    def around_end(k):
        i = AROUND.index(k)
        return remote(row(relay_b, i), row(rin, k), c_send.at[i], r_recv.at[k], down_x)

    low_edge = remote(row(vort, 0), vup, h_send.at[0], h_recv.at[0], preceding)
    high_edge = remote(row(comb, rows_az), row(comb, 0), h_send.at[1], h_recv.at[1], following)
    edges = remote(edge_s, edge_r, h_send.at[2], h_recv.at[2], following)

    def radial(side, device):
        return remote(
            edge_out.at[side], edge_in.at[side], e_send.at[side], e_recv.at[side], device
        )

    capacity = tbuf.shape[0] // n_ra
    group = 2 * capacity

    def tile_copy(d):
        to = (chip + d) % n_chip
        return remote(
            sbuf.at[pl.ds(pl.multiple_of(to * group, group), group)], trecv.at[chip],
            t_send.at[d], t_recv.at[d], (j, to * 2 + core),
        )

    exchange = remote(trecv, tsib, t_send.at[0], t_recv.at[0], sibling)

    def start_row(k):
        if k in THROUGH:
            pl.when(last)(lambda: through(k).start())
            pl.when(jnp.logical_not(last))(lambda: straight(k).start())
        else:
            straight(k).start()

    start_row(7)
    around(AROUND[0]).start()
    edges.start()
    start_row(0)
    around(AROUND[1]).start()
    low_edge.start()
    for k in STRAIGHT[2:]:
        start_row(k)

    pl.when(z_low)(lambda: pl.semaphore_wait(up_sem, 1))
    pl.when(z_high)(
        lambda: pl.semaphore_signal(up_sem, inc=1, device_id=above, device_id_type=MESH)
    )

    loads[2].wait()
    loads[3].wait()
    loads[4].wait()
    slots = tbuf.shape[0]
    slot = lax.broadcasted_iota(jnp.int32, (slots, slots), 0)
    lane = lax.broadcasted_iota(jnp.int32, (slots, slots), 1)
    ids = jnp.broadcast_to(idbuf[...].astype(jnp.float32), (slots, slots))
    id_col = jnp.sum(jnp.where(slot == lane, ids, 0.0), axis=1, keepdims=True)
    slot_n = lax.broadcasted_iota(jnp.int32, (slots, n_ra), 0)
    lane_n = lax.broadcasted_iota(jnp.int32, (slots, n_ra), 1)
    counts = jnp.broadcast_to(cntbuf[...].astype(jnp.float32), (slots, n_ra))
    count_col = jnp.sum(
        jnp.where(slot_n // capacity == lane_n, counts, 0.0), axis=1, keepdims=True
    )
    used = (slot % capacity).astype(jnp.float32) < count_col
    width = tbuf.shape[1]
    sbuf[:, :width] = tbuf[...]
    sbuf[:, width:] = jnp.where(used, id_col, -1.0)
    trecv[pl.ds(chip, 1)] = sbuf[pl.ds(pl.multiple_of(chip * group, group), group)][None]

    def send_tiles(low_z, high_z):
        @pl.when(jnp.logical_and(z >= low_z, z <= high_z))
        def _():
            pl.when(z_high)(lambda: pl.semaphore_wait(down_sem, 1))
            pl.when(z_low)(
                lambda: pl.semaphore_signal(down_sem, inc=1, device_id=below, device_id_type=MESH)
            )
            for d in range(1, n_chip):
                tile_copy(d).start()

    def take(k):
        straight(k).wait_recv()
        for c in range(3):
            comb[c, k + 1] = vbuf[c, k] + rin[c, k].astype(jnp.float32)

    def relay_through(k):
        @pl.when(first)
        def _():
            through(k).wait_recv()
            through_on(k).start()

    def relay_first(k):
        around(k).wait_recv()
        pl.when(x == 2)(lambda: around_on(k, at(1, y + 1)).start())
        pl.when(x != 2)(lambda: around_on(k, down_x).start())

    def relay_second(k):
        around_on(k, down_x).wait_recv()
        around_end(k).start()

    send_tiles(n_z - 3, n_z - 1)
    loads[1].wait()
    for c in range(3):
        for k in range(rows_az):
            edge_out[1, c, k : k + 1] = vbuf[c, k, :1]
            edge_out[0, c, k : k + 1] = vbuf[c, k, rows_rad - 1 :]

    @pl.when(jnp.logical_not(has_low))
    def _():
        edge_in[0] = jnp.zeros_like(edge_in[0])

    @pl.when(jnp.logical_not(has_high))
    def _():
        edge_in[1] = jnp.zeros_like(edge_in[1])

    relay_first(AROUND[0])
    take(7)
    high_edge.start()
    relay_through(0)
    relay_first(AROUND[1])
    edges.wait_recv()
    for c in range(3):
        arrived = edge_r[c].astype(jnp.float32)
        edge_out[1, c] += arrived[:rows_az]
        edge_out[0, c] += arrived[rows_az:]
    in_run_low = jnp.logical_and(has_low, jnp.logical_not(seam_low))
    in_run_high = jnp.logical_and(has_high, jnp.logical_not(seam_high))
    pl.when(in_run_high)(lambda: radial(0, higher).start())
    pl.when(in_run_low)(lambda: radial(1, lower).start())
    send_tiles(3, n_z - 4)
    relay_second(AROUND[0])
    relay_through(1)
    take(0)
    relay_second(AROUND[1])
    relay_through(2)
    take(1)
    relay_through(6)
    send_tiles(0, 2)
    take(2)
    relay_through(5)
    for d in range(1, n_chip):
        tile_copy(d).wait_recv()
    exchange.start()
    pl.when(seam_high)(lambda: radial(0, higher).start())
    pl.when(seam_low)(lambda: radial(1, lower).start())

    axial = lax.broadcasted_iota(jnp.int32, (rows_rad, cells_ax), 1)
    radial_row = lax.broadcasted_iota(jnp.int32, (rows_rad, cells_ax), 0)
    position = (r * rows_rad + radial_row).astype(jnp.float32)
    inverse = 1.0 / (0.5 + (position + 0.5) / (rows_rad * n_ra))
    inverse_sq = inverse * inverse

    def stencil(k):
        v0 = cbuf[0, k].astype(jnp.float32)
        v1 = cbuf[1, k].astype(jnp.float32)
        v2 = cbuf[2, k].astype(jnp.float32)
        rad = (0.25 * DIFFUSION) * inverse - 0.5 * v0
        azi_even = DIFFUSION * inverse_sq
        azi_odd = 0.5 * v1 * inverse
        axi = 0.5 * v2
        middle = (1.0 - 4.0 * DIFFUSION) - (2.0 * DIFFUSION) * inverse_sq
        turn = (0.5 * DIFFUSION) * inverse_sq
        for c in range(3):
            f = comb[c, k + 1]
            nxt, prv = comb[c, k + 2], comb[c, k]
            up = pltpu.roll(f, rows_rad - 1, 0)
            up = jnp.where(radial_row == rows_rad - 1, edge_in[1, c, k : k + 1], up)
            down = pltpu.roll(f, 1, 0)
            down = jnp.where(radial_row == 0, edge_in[0, c, k : k + 1], down)
            right = jnp.where(axial == cells_ax - 1, 0.0, pltpu.roll(f, cells_ax - 1, 1))
            left = jnp.where(axial == 0, 0.0, pltpu.roll(f, 1, 1))
            total = middle * f + src[c, k]
            total = total + DIFFUSION * ((up + down) + (right + left))
            total = total + rad * (up - down) - axi * (right - left)
            total = total + azi_even * (nxt + prv) - azi_odd * (nxt - prv)
            if c == 0:
                total = total - (0.5 * turn) * f - turn * (comb[1, k + 2] - comb[1, k])
            elif c == 1:
                total = total - (0.5 * turn) * f + turn * (comb[0, k + 2] - comb[0, k])
            obuf[c, k] = total

    def finish(k):
        stencil(k)
        pltpu.make_async_copy(row(obuf, k), row(out, k), osem.at[k]).start()

    exchange.wait_recv()
    keep = (slot % group) // capacity == core
    halves = []
    for i, got in enumerate((trecv, tsib)):
        part = got[...].reshape(slots, width + slots)
        value = part[:, :width]
        top = value.astype(jnp.bfloat16)
        tmat[i * slots : (i + 1) * slots] = top
        tmat[(2 + i) * slots : (3 + i) * slots] = (value - top.astype(jnp.float32)).astype(
            jnp.bfloat16
        )
        halves.append(jnp.where(keep, part[:, width:], -1.0).T)
    blocks = jnp.concatenate(halves, axis=1)
    m = lax.broadcasted_iota(jnp.int32, blocks.shape, 0)
    per_row = cells_ax // TS
    local_block = (m % rows_rad) * per_row + m // rows_rad
    for a in range(rows_az):
        wanted = (local_block + a * rows_rad * per_row).astype(jnp.float32)
        hot = jnp.where(blocks == wanted, 1.0, 0.0).astype(jnp.bfloat16)
        placed = jnp.dot(
            jnp.concatenate([hot, hot], axis=1), tmat[...], preferred_element_type=jnp.float32
        )
        for b in range(per_row):
            for c in range(3):
                src[c, a, :, b * TS : (b + 1) * TS] = placed[
                    b * rows_rad : (b + 1) * rows_rad, c * TS : (c + 1) * TS
                ]

    loads[5].wait()
    low_edge.wait_recv()
    for c in range(3):
        comb[c, rows_az + 1] = vup[c, 0] + rbuf[c, 0].astype(jnp.float32)
    high_edge.wait_recv()
    pl.when(has_low)(lambda: radial(0, (j, r)).wait_recv())
    pl.when(has_high)(lambda: radial(1, (j, r)).wait_recv())
    finish(0)
    finish(1)
    take(3)
    finish(2)
    take(4)
    finish(3)
    take(6)
    finish(7)
    take(5)
    finish(4)
    finish(5)
    finish(6)

    for k in STRAIGHT:
        straight(k).wait_send()
    for k in AROUND:
        around(k).wait_send()
        around_on(k, down_x).wait_send()
        around_end(k).wait_send()

    @pl.when(first)
    def _():
        for k in THROUGH:
            through_on(k).wait_send()

    low_edge.wait_send()
    high_edge.wait_send()
    edges.wait_send()
    pl.when(has_high)(lambda: radial(0, (j, r)).wait_send())
    pl.when(has_low)(lambda: radial(1, (j, r)).wait_send())
    for d in range(1, n_chip):
        tile_copy(d).wait_send()
    exchange.wait_send()
    for k in range(rows_az):
        pltpu.make_async_copy(row(obuf, k), row(out, k), osem.at[k]).wait()


def body(vorticity, rotor_field, courant, load_tiles, tile_block, tile_count):
    shape = vorticity.shape
    _, rows_az, rows_rad, cells_ax = shape
    slots, width = load_tiles.shape[2:]
    n_ra = lax.axis_size("ra")
    n_chip = n_ra // 2
    group = slots // n_chip
    one_row = (3, 1, rows_rad, cells_ax)

    def relay(n):
        return pltpu.VMEM((3, n, rows_rad, cells_ax), jnp.bfloat16)

    dma = pltpu.SemaphoreType.DMA
    around, through = len(AROUND), len(THROUGH)
    scratch = [
        pltpu.VMEM(shape, jnp.float32),
        pltpu.VMEM(shape, jnp.bfloat16),
        pltpu.VMEM(shape, jnp.bfloat16),
        pltpu.VMEM(shape, jnp.bfloat16),
        pltpu.VMEM((3, rows_az + 2, rows_rad, cells_ax), jnp.float32),
        pltpu.VMEM(shape, jnp.float32),
        pltpu.VMEM(shape, jnp.float32),
        pltpu.VMEM(one_row, jnp.float32),
        relay(around),
        relay(around),
        relay(through),
        pltpu.VMEM((3, 2 * rows_az, cells_ax), jnp.float32),
        pltpu.VMEM((3, 2 * rows_az, cells_ax), jnp.bfloat16),
        pltpu.VMEM((3, 2 * rows_az, cells_ax), jnp.bfloat16),
        pltpu.VMEM((2, 3, rows_az, cells_ax), jnp.float32),
        pltpu.VMEM((2, 3, rows_az, cells_ax), jnp.float32),
        pltpu.VMEM((slots, width), jnp.float32),
        pltpu.VMEM((1, slots), jnp.int32),
        pltpu.VMEM((1, n_ra), jnp.int32),
        pltpu.VMEM((slots, width + slots), jnp.float32),
        pltpu.VMEM((n_chip, group, width + slots), jnp.float32),
        pltpu.VMEM((n_chip, group, width + slots), jnp.float32),
        pltpu.VMEM((4 * slots, width), jnp.bfloat16),
        dma((6,)),
        dma((rows_az,)),
        dma((rows_az,)),
        dma((rows_az,)),
        dma((around,)),
        dma((around,)),
        dma((around,)),
        dma((around,)),
        dma((around,)),
        dma((through,)),
        dma((through,)),
        dma((3,)),
        dma((3,)),
        dma((2,)),
        dma((2,)),
        dma((n_chip,)),
        dma((n_chip,)),
        pltpu.SemaphoreType.REGULAR,
        pltpu.SemaphoreType.REGULAR,
    ]
    return pl.pallas_call(
        kernel,
        name="step",
        out_shape=jax.ShapeDtypeStruct(shape, jnp.float32),
        in_specs=[pl.BlockSpec(memory_space=pltpu.HBM)] * 6,
        out_specs=pl.BlockSpec(memory_space=pl.ANY),
        scratch_shapes=scratch,
        compiler_params=pltpu.CompilerParams(
            collective_id=0, has_side_effects=True, vmem_limit_bytes=62 * 1024 * 1024
        ),
    )(vorticity, rotor_field, courant, load_tiles, tile_block, tile_count)


def solution(mesh):
    in_specs = (
        P(None, "azi", "ra", None),
        P(None, "azi", "ra", None),
        P(None, "azi", "ra", None),
        P("azi", "ra", None, None),
        P("azi", "ra", None),
        P("azi", "ra", None),
    )
    out_specs = P(None, "azi", "ra", None)
    return jax.shard_map(body, mesh=mesh, in_specs=in_specs, out_specs=out_specs, check_vma=False)
```

time: 63.8 us -> 52.2 us (0.82)
  the two profiles are of different devices: /device:TPU:24 before, /device:TPU:40 now
where the time goes in v2:
time: 52.2 us; the launch traced here: 52 us
  Pallas kernels  49.3 us (94%)
  local copies, waits for them, and re-layouts  2.73 us (5%)
    pallas_call x1, Pallas kernels, body(): pl.pallas_call(kernel, name='step', out_shape=jax.ShapeDtypeStruct(shape,...  49.3 us
    unnamed x1, local copies, waits for them, and re-layouts  2.73 us

profile of v2, /device:TPU:40, one launch (start us, length us, event | category | flops | bytes accessed | tf_op | source)
XLA Modules:
  0.0 52.0 jit_solution(12619669481326283338)
XLA Ops:
  0.0 49.3 %step.1 = f32[3,8,16,1024]{3,2,1,0:T(8,128)} custom-call(f32[3,8,16,1024]{3,2,1,0:T(8,128)} %vort.1, bf16[3,8,16,1024]{3,2,1,0:T(8,128)(2,1)} %rotor.1, bf16[3,8,16,1024]{3,2,1,0:T(8,128)(2,1)} %cour.1, f32[1,1,128,384]{3,2,1,0:T(8,128)} %tiles.1, s32[1,1,128]{2,1,0:T(1,128)} %tile_id.1, s32[1,1,32]{2,1,0:T(1,128)} %tile_n.1), custom_call_target="tpu_custom_call" | custom-call | tf_op jit(solution)/shard_map/step/pallas_call | solution.py:446
  49.3 2.7 %copy.8 = f32[3,8,16,1024]{3,2,1,0:T(8,128)} copy(f32[3,8,16,1024]{3,2,1,0:T(8,128)} %step.1) | data formatting | bytes 3145728

commit v3 on v2

--- a/solution.py
+++ b/solution.py
@@ -12,17 +12,18 @@
 MESH = pl.DeviceIdType.MESH
 CHIP_X = 4
 
-AROUND = (3, 4)
-THROUGH = (0, 1, 2, 6, 5)
-STRAIGHT = (7, 0, 1, 2, 6, 5)
+AROUND = (3, 4, 5)
+AROUND_LAST = 5
+THROUGH = (0, 1, 2, 6)
+STRAIGHT = (0, 7, 5, 1, 2, 6)
 
 
 def kernel(
     vort, rotor, cour, tiles, tile_id, tile_n, out,
-    vbuf, cbuf, rbuf, rin, comb, obuf, src, vup,
+    vbuf, cbuf, rbuf, rin, comb, src, vup,
     relay_a, relay_b, relay_p, edge_f, edge_s, edge_r, edge_out, edge_in,
     tbuf, idbuf, cntbuf, sbuf, trecv, tsib, tmat,
-    lsem, osem, r_send, r_recv, a_send, a_recv, b_send, b_recv, c_send,
+    lsem, r_send, r_recv, a_send, a_recv, b_send, b_recv, c_send,
     p_recv, q_send, h_send, h_recv, e_send, e_recv, t_send, t_recv, up_sem, down_sem,
 ):
     n_azi, n_ra = lax.axis_size("azi"), lax.axis_size("ra")
@@ -158,20 +159,23 @@
     exchange = remote(trecv, tsib, t_send.at[0], t_recv.at[0], sibling)
 
     def start_row(k):
-        if k in THROUGH:
-            pl.when(last)(lambda: through(k).start())
+        if k in THROUGH or k == AROUND_LAST:
+            other_way = around if k == AROUND_LAST else through
+            pl.when(last)(lambda: other_way(k).start())
             pl.when(jnp.logical_not(last))(lambda: straight(k).start())
         else:
             straight(k).start()
 
+    start_row(0)
     start_row(7)
-    around(AROUND[0]).start()
+    around(3).start()
+    start_row(5)
     edges.start()
-    start_row(0)
-    around(AROUND[1]).start()
+    around(4).start()
+    start_row(1)
     low_edge.start()
-    for k in STRAIGHT[2:]:
-        start_row(k)
+    start_row(2)
+    start_row(6)
 
     pl.when(z_low)(lambda: pl.semaphore_wait(up_sem, 1))
     pl.when(z_high)(
@@ -228,7 +232,7 @@
         around_on(k, down_x).wait_recv()
         around_end(k).start()
 
-    send_tiles(n_z - 3, n_z - 1)
+    send_tiles(n_z - 2, n_z - 1)
     loads[1].wait()
     for c in range(3):
         for k in range(rows_az):
@@ -243,11 +247,15 @@
     def _():
         edge_in[1] = jnp.zeros_like(edge_in[1])
 
-    relay_first(AROUND[0])
+    relay_through(0)
+    relay_first(3)
     take(7)
     high_edge.start()
-    relay_through(0)
-    relay_first(AROUND[1])
+    send_tiles(n_z - 3, n_z - 3)
+    relay_through(1)
+    pl.when(x == 2)(lambda: relay_first(5))
+    relay_first(4)
+    relay_through(2)
     edges.wait_recv()
     for c in range(3):
         arrived = edge_r[c].astype(jnp.float32)
@@ -258,21 +266,30 @@
     pl.when(in_run_high)(lambda: radial(0, higher).start())
     pl.when(in_run_low)(lambda: radial(1, lower).start())
     send_tiles(3, n_z - 4)
-    relay_second(AROUND[0])
-    relay_through(1)
+    relay_through(6)
+    relay_second(3)
+    pl.when(x == 1)(lambda: relay_second(5))
+    relay_second(4)
+    send_tiles(0, 2)
     take(0)
-    relay_second(AROUND[1])
-    relay_through(2)
     take(1)
-    relay_through(6)
-    send_tiles(0, 2)
-    take(2)
-    relay_through(5)
-    for d in range(1, n_chip):
+    take(5)
+
+    @pl.when(seam_high)
+    def _():
+        tile_copy(n_chip - 1).wait_recv()
+        radial(0, higher).start()
+
+    @pl.when(seam_low)
+    def _():
+        tile_copy(1).wait_recv()
+        radial(1, lower).start()
+
+    pl.when(jnp.logical_not(seam_high))(lambda: tile_copy(n_chip - 1).wait_recv())
+    pl.when(jnp.logical_not(seam_low))(lambda: tile_copy(1).wait_recv())
+    for d in range(2, n_chip - 1):
         tile_copy(d).wait_recv()
     exchange.start()
-    pl.when(seam_high)(lambda: radial(0, higher).start())
-    pl.when(seam_low)(lambda: radial(1, lower).start())
 
     axial = lax.broadcasted_iota(jnp.int32, (rows_rad, cells_ax), 1)
     radial_row = lax.broadcasted_iota(jnp.int32, (rows_rad, cells_ax), 0)
@@ -307,11 +324,7 @@
                 total = total - (0.5 * turn) * f - turn * (comb[1, k + 2] - comb[1, k])
             elif c == 1:
                 total = total - (0.5 * turn) * f + turn * (comb[0, k + 2] - comb[0, k])
-            obuf[c, k] = total
-
-    def finish(k):
-        stencil(k)
-        pltpu.make_async_copy(row(obuf, k), row(out, k), osem.at[k]).start()
+            out[c, k] = total
 
     exchange.wait_recv()
     keep = (slot % group) // capacity == core
@@ -348,25 +361,31 @@
     high_edge.wait_recv()
     pl.when(has_low)(lambda: radial(0, (j, r)).wait_recv())
     pl.when(has_high)(lambda: radial(1, (j, r)).wait_recv())
-    finish(0)
-    finish(1)
+    stencil(0)
     take(3)
-    finish(2)
     take(4)
-    finish(3)
+    stencil(4)
+    take(2)
+    stencil(1)
+    stencil(2)
+    stencil(3)
     take(6)
-    finish(7)
-    take(5)
-    finish(4)
-    finish(5)
-    finish(6)
+    stencil(7)
+    stencil(5)
+    stencil(6)
 
     for k in STRAIGHT:
-        straight(k).wait_send()
+        if k != AROUND_LAST:
+            straight(k).wait_send()
     for k in AROUND:
-        around(k).wait_send()
-        around_on(k, down_x).wait_send()
-        around_end(k).wait_send()
+        if k != AROUND_LAST:
+            around(k).wait_send()
+            around_on(k, down_x).wait_send()
+            around_end(k).wait_send()
+    pl.when(last)(lambda: around(AROUND_LAST).wait_send())
+    pl.when(jnp.logical_not(last))(lambda: straight(AROUND_LAST).wait_send())
+    pl.when(x == 2)(lambda: around_on(AROUND_LAST, down_x).wait_send())
+    pl.when(x == 1)(lambda: around_end(AROUND_LAST).wait_send())
 
     @pl.when(first)
     def _():
@@ -381,8 +400,6 @@
     for d in range(1, n_chip):
         tile_copy(d).wait_send()
     exchange.wait_send()
-    for k in range(rows_az):
-        pltpu.make_async_copy(row(obuf, k), row(out, k), osem.at[k]).wait()
 
 
 def body(vorticity, rotor_field, courant, load_tiles, tile_block, tile_count):
@@ -405,7 +422,6 @@
         pltpu.VMEM(shape, jnp.bfloat16),
         pltpu.VMEM(shape, jnp.bfloat16),
         pltpu.VMEM((3, rows_az + 2, rows_rad, cells_ax), jnp.float32),
-        pltpu.VMEM(shape, jnp.float32),
         pltpu.VMEM(shape, jnp.float32),
         pltpu.VMEM(one_row, jnp.float32),
         relay(around),
@@ -424,7 +440,6 @@
         pltpu.VMEM((n_chip, group, width + slots), jnp.float32),
         pltpu.VMEM((4 * slots, width), jnp.bfloat16),
         dma((6,)),
-        dma((rows_az,)),
         dma((rows_az,)),
         dma((rows_az,)),
         dma((around,)),
@@ -446,9 +461,9 @@
     return pl.pallas_call(
         kernel,
         name="step",
-        out_shape=jax.ShapeDtypeStruct(shape, jnp.float32),
+        out_shape=pltpu.VMEM(shape, jnp.float32),
         in_specs=[pl.BlockSpec(memory_space=pltpu.HBM)] * 6,
-        out_specs=pl.BlockSpec(memory_space=pl.ANY),
+        out_specs=pl.BlockSpec(memory_space=pltpu.VMEM),
         scratch_shapes=scratch,
         compiler_params=pltpu.CompilerParams(
             collective_id=0, has_side_effects=True, vmem_limit_bytes=62 * 1024 * 1024

time: 52.2 us -> 44.9 us (0.86)
  the two profiles are of different devices: /device:TPU:40 before, /device:TPU:8 now
where the time goes in v3:
time: 44.9 us; the launch traced here: 44.8 us
  Pallas kernels  43.6 us (97%)
  local copies, waits for them, and re-layouts  1.15 us (3%)
    pallas_call x1, Pallas kernels, body(): pl.pallas_call(kernel, name='step', out_shape=pltpu.VMEM(shape, jnp.float...  43.6 us
    unnamed x1, local copies, waits for them, and re-layouts  1.15 us

profile of v3, /device:TPU:8, one launch (start us, length us, event | category | flops | bytes accessed | tf_op | source)
XLA Modules:
  0.0 44.8 jit_solution(15325151808182887624)
XLA Ops:
  0.0 43.6 %step.1 = f32[3,8,16,1024]{3,2,1,0:T(8,128)S(1)} custom-call(f32[3,8,16,1024]{3,2,1,0:T(8,128)} %vort.1, bf16[3,8,16,1024]{3,2,1,0:T(8,128)(2,1)} %rotor.1, bf16[3,8,16,1024]{3,2,1,0:T(8,128)(2,1)} %cour.1, f32[1,1,128,384]{3,2,1,0:T(8,128)} %tiles.1, s32[1,1,128]{2,1,0:T(1,128)} %tile_id.1, s32[1,1,32]{2,1,0:T(1,128)} %tile_n.1), custom_call_target="tpu_custom_call" | custom-call | tf_op jit(solution)/shard_map/step/pallas_call | solution.py:461
  43.7 1.1 %copy.8 = f32[3,8,16,1024]{3,2,1,0:T(8,128)} copy(f32[3,8,16,1024]{3,2,1,0:T(8,128)S(1)} %step.1) | data formatting | bytes 3145728

commit v4 on v3

--- a/solution.py
+++ b/solution.py
@@ -24,7 +24,7 @@
     relay_a, relay_b, relay_p, edge_f, edge_s, edge_r, edge_out, edge_in,
     tbuf, idbuf, cntbuf, sbuf, trecv, tsib, tmat,
     lsem, r_send, r_recv, a_send, a_recv, b_send, b_recv, c_send,
-    p_recv, q_send, h_send, h_recv, e_send, e_recv, t_send, t_recv, up_sem, down_sem,
+    p_recv, q_send, h_send, h_recv, e_send, e_recv, t_send, t_recv, up_sem, down_sem, seam_sem,
 ):
     n_azi, n_ra = lax.axis_size("azi"), lax.axis_size("ra")
     n_y = n_azi // CHIP_X
@@ -84,19 +84,87 @@
     pl.when(first)(lambda: greet(down_x))
     pl.when(x == 2)(lambda: greet(at(1, y + 1)))
     pl.when(x == 1)(lambda: greet(at(2, y + n_y - 1)))
+    pl.when(x == 1)(lambda: greet(at(0, y + 1)))
 
     @pl.when(first)
     def _():
         greet(up_y)
         greet(down_y)
+        greet(at(1, y + n_y - 1))
 
     pl.when(z_high)(lambda: greet(above))
     pl.when(z_low)(lambda: greet(below))
     pl.when(near_low)(lambda: greet(lower))
     pl.when(near_high)(lambda: greet(higher))
-    others = 5 + 2 * first.astype(jnp.int32)
+    others = 5 + 3 * first.astype(jnp.int32) + (x == 1).astype(jnp.int32)
     for near in (z_high, z_low, near_low, near_high):
         others = others + near.astype(jnp.int32)
+
+    pl.semaphore_wait(bar, others)
+
+    def remote(source, target, send, recv, device):
+        return pltpu.make_async_remote_copy(
+            src_ref=source, dst_ref=target, send_sem=send, recv_sem=recv,
+            device_id=device, device_id_type=MESH,
+        )
+
+    def straight(k):
+        return remote(row(rotor, k), row(rin, k), r_send.at[k], r_recv.at[k], following)
+
+    def through(k):
+        i = THROUGH.index(k)
+        return remote(row(rotor, k), row(relay_p, i), r_send.at[k], p_recv.at[i], up_x)
+
+    def through_on(k):
+        i = THROUGH.index(k)
+        return remote(row(relay_p, i), row(rin, k), q_send.at[i], r_recv.at[k], up_y)
+
+    def around(k):
+        i = AROUND.index(k)
+        return remote(row(rotor, k), row(relay_a, i), a_send.at[i], a_recv.at[i], down_x)
+
+    def around_on(k, device):
+        i = AROUND.index(k)
+        return remote(row(relay_a, i), row(relay_b, i), b_send.at[i], b_recv.at[i], device)
+
+    def around_end(k, device):
+        i = AROUND.index(k)
+        return remote(row(relay_b, i), row(rin, k), c_send.at[i], r_recv.at[k], device)
+
+    low_edge = remote(row(vort, 0), vup, h_send.at[0], h_recv.at[0], preceding)
+    high_edge = remote(row(comb, rows_az), row(comb, 0), h_send.at[1], h_recv.at[1], following)
+    edges = remote(edge_s, edge_r, h_send.at[2], h_recv.at[2], following)
+
+    def radial(side, device):
+        return remote(
+            edge_out.at[side], edge_in.at[side], e_send.at[side], e_recv.at[side], device
+        )
+
+    capacity = tbuf.shape[0] // n_ra
+    group = 2 * capacity
+
+    def tile_copy(d):
+        to = (chip + d) % n_chip
+        return remote(
+            sbuf.at[pl.ds(pl.multiple_of(to * group, group), group)], trecv.at[chip],
+            t_send.at[d], t_recv.at[d], (j, to * 2 + core),
+        )
+
+    exchange = remote(trecv, tsib, t_send.at[0], t_recv.at[0], sibling)
+
+    def start_row(k):
+        if k in THROUGH or k == AROUND_LAST:
+            other_way = around if k == AROUND_LAST else through
+            pl.when(last)(lambda: other_way(k).start())
+            pl.when(jnp.logical_not(last))(lambda: straight(k).start())
+        else:
+            straight(k).start()
+
+    start_row(0)
+    start_row(7)
+    around(3).start()
+    start_row(5)
+    around(4).start()
 
     loads[0].wait()
     for c in range(3):
@@ -105,73 +173,7 @@
             edge_f[c, k : k + 1] = whole[:1]
             edge_f[c, rows_az + k : rows_az + k + 1] = whole[rows_rad - 1 :]
     edge_s[...] = edge_f[...].astype(jnp.bfloat16)
-
-    pl.semaphore_wait(bar, others)
-
-    def remote(source, target, send, recv, device):
-        return pltpu.make_async_remote_copy(
-            src_ref=source, dst_ref=target, send_sem=send, recv_sem=recv,
-            device_id=device, device_id_type=MESH,
-        )
-
-    def straight(k):
-        return remote(row(rotor, k), row(rin, k), r_send.at[k], r_recv.at[k], following)
-
-    def through(k):
-        i = THROUGH.index(k)
-        return remote(row(rotor, k), row(relay_p, i), r_send.at[k], p_recv.at[i], up_x)
-
-    def through_on(k):
-        i = THROUGH.index(k)
-        return remote(row(relay_p, i), row(rin, k), q_send.at[i], r_recv.at[k], up_y)
-
-    def around(k):
-        i = AROUND.index(k)
-        return remote(row(rotor, k), row(relay_a, i), a_send.at[i], a_recv.at[i], down_x)
-
-    def around_on(k, device):
-        i = AROUND.index(k)
-        return remote(row(relay_a, i), row(relay_b, i), b_send.at[i], b_recv.at[i], device)
-
-    def around_end(k):
-        i = AROUND.index(k)
-        return remote(row(relay_b, i), row(rin, k), c_send.at[i], r_recv.at[k], down_x)
-
-    low_edge = remote(row(vort, 0), vup, h_send.at[0], h_recv.at[0], preceding)
-    high_edge = remote(row(comb, rows_az), row(comb, 0), h_send.at[1], h_recv.at[1], following)
-    edges = remote(edge_s, edge_r, h_send.at[2], h_recv.at[2], following)
-
-    def radial(side, device):
-        return remote(
-            edge_out.at[side], edge_in.at[side], e_send.at[side], e_recv.at[side], device
-        )
-
-    capacity = tbuf.shape[0] // n_ra
-    group = 2 * capacity
-
-    def tile_copy(d):
-        to = (chip + d) % n_chip
-        return remote(
-            sbuf.at[pl.ds(pl.multiple_of(to * group, group), group)], trecv.at[chip],
-            t_send.at[d], t_recv.at[d], (j, to * 2 + core),
-        )
-
-    exchange = remote(trecv, tsib, t_send.at[0], t_recv.at[0], sibling)
-
-    def start_row(k):
-        if k in THROUGH or k == AROUND_LAST:
-            other_way = around if k == AROUND_LAST else through
-            pl.when(last)(lambda: other_way(k).start())
-            pl.when(jnp.logical_not(last))(lambda: straight(k).start())
-        else:
-            straight(k).start()
-
-    start_row(0)
-    start_row(7)
-    around(3).start()
-    start_row(5)
     edges.start()
-    around(4).start()
     start_row(1)
     low_edge.start()
     start_row(2)
@@ -180,6 +182,18 @@
     pl.when(z_low)(lambda: pl.semaphore_wait(up_sem, 1))
     pl.when(z_high)(
         lambda: pl.semaphore_signal(up_sem, inc=1, device_id=above, device_id_type=MESH)
+    )
+    @pl.when(jnp.logical_not(z_high))
+    def _():
+        for d in range(1, n_z):
+            pl.semaphore_signal(down_sem, inc=1, device_id=(j, r - 2 * d), device_id_type=MESH)
+
+    top = jnp.logical_and(core == 1, z == n_z - 1)
+    tell = jnp.logical_and(top, chip >= n_z)
+    pl.when(tell)(
+        lambda: pl.semaphore_signal(
+            seam_sem, inc=1, device_id=(j, r - n_ra // 2), device_id_type=MESH
+        )
     )
 
     loads[2].wait()
@@ -206,9 +220,6 @@
         @pl.when(jnp.logical_and(z >= low_z, z <= high_z))
         def _():
             pl.when(z_high)(lambda: pl.semaphore_wait(down_sem, 1))
-            pl.when(z_low)(
-                lambda: pl.semaphore_signal(down_sem, inc=1, device_id=below, device_id_type=MESH)
-            )
             for d in range(1, n_chip):
                 tile_copy(d).start()
 
@@ -225,12 +236,15 @@
 
     def relay_first(k):
         around(k).wait_recv()
-        pl.when(x == 2)(lambda: around_on(k, at(1, y + 1)).start())
-        pl.when(x != 2)(lambda: around_on(k, down_x).start())
+        if k == AROUND_LAST:
+            around_on(k, down_x).start()
+        else:
+            pl.when(x == 2)(lambda: around_on(k, at(1, y + 1)).start())
+            pl.when(x != 2)(lambda: around_on(k, down_x).start())
 
     def relay_second(k):
         around_on(k, down_x).wait_recv()
-        around_end(k).start()
+        around_end(k, at(0, y + 1) if k == AROUND_LAST else down_x).start()
 
     send_tiles(n_z - 2, n_z - 1)
     loads[1].wait()
@@ -251,7 +265,7 @@
     relay_first(3)
     take(7)
     high_edge.start()
-    send_tiles(n_z - 3, n_z - 3)
+    send_tiles(n_z - 4, n_z - 3)
     relay_through(1)
     pl.when(x == 2)(lambda: relay_first(5))
     relay_first(4)
@@ -262,32 +276,25 @@
         edge_out[1, c] += arrived[:rows_az]
         edge_out[0, c] += arrived[rows_az:]
     in_run_low = jnp.logical_and(has_low, jnp.logical_not(seam_low))
-    in_run_high = jnp.logical_and(has_high, jnp.logical_not(seam_high))
-    pl.when(in_run_high)(lambda: radial(0, higher).start())
+    pl.when(seam_high)(lambda: pl.semaphore_wait(seam_sem, 1))
+    pl.when(has_high)(lambda: radial(0, higher).start())
     pl.when(in_run_low)(lambda: radial(1, lower).start())
-    send_tiles(3, n_z - 4)
+    send_tiles(0, n_z - 5)
     relay_through(6)
     relay_second(3)
     pl.when(x == 1)(lambda: relay_second(5))
     relay_second(4)
-    send_tiles(0, 2)
     take(0)
     take(1)
     take(5)
 
-    @pl.when(seam_high)
-    def _():
-        tile_copy(n_chip - 1).wait_recv()
-        radial(0, higher).start()
-
     @pl.when(seam_low)
     def _():
         tile_copy(1).wait_recv()
         radial(1, lower).start()
 
-    pl.when(jnp.logical_not(seam_high))(lambda: tile_copy(n_chip - 1).wait_recv())
     pl.when(jnp.logical_not(seam_low))(lambda: tile_copy(1).wait_recv())
-    for d in range(2, n_chip - 1):
+    for d in range(2, n_chip):
         tile_copy(d).wait_recv()
     exchange.start()
 
@@ -381,11 +388,11 @@
         if k != AROUND_LAST:
             around(k).wait_send()
             around_on(k, down_x).wait_send()
-            around_end(k).wait_send()
+            around_end(k, down_x).wait_send()
     pl.when(last)(lambda: around(AROUND_LAST).wait_send())
     pl.when(jnp.logical_not(last))(lambda: straight(AROUND_LAST).wait_send())
     pl.when(x == 2)(lambda: around_on(AROUND_LAST, down_x).wait_send())
-    pl.when(x == 1)(lambda: around_end(AROUND_LAST).wait_send())
+    pl.when(x == 1)(lambda: around_end(AROUND_LAST, down_x).wait_send())
 
     @pl.when(first)
     def _():
@@ -457,6 +464,7 @@
         dma((n_chip,)),
         pltpu.SemaphoreType.REGULAR,
         pltpu.SemaphoreType.REGULAR,
+        pltpu.SemaphoreType.REGULAR,
     ]
     return pl.pallas_call(
         kernel,

time: 44.9 us -> 41.7 us (0.929)
  the two profiles are of different devices: /device:TPU:8 before, /device:TPU:57 now
where the time goes in v4:
time: 41.7 us; the launch traced here: 41.6 us
  Pallas kernels  40.5 us (97%)
  local copies, waits for them, and re-layouts  1.15 us (3%)
    pallas_call x1, Pallas kernels, body(): pl.pallas_call(kernel, name='step', out_shape=pltpu.VMEM(shape, jnp.float...  40.5 us
    unnamed x1, local copies, waits for them, and re-layouts  1.15 us

profile of v4, /device:TPU:57, one launch (start us, length us, event | category | flops | bytes accessed | tf_op | source)
XLA Modules:
  0.0 41.6 jit_solution(8107460105966145805)
XLA Ops:
  0.0 40.5 %step.1 = f32[3,8,16,1024]{3,2,1,0:T(8,128)S(1)} custom-call(f32[3,8,16,1024]{3,2,1,0:T(8,128)} %vort.1, bf16[3,8,16,1024]{3,2,1,0:T(8,128)(2,1)} %rotor.1, bf16[3,8,16,1024]{3,2,1,0:T(8,128)(2,1)} %cour.1, f32[1,1,128,384]{3,2,1,0:T(8,128)} %tiles.1, s32[1,1,128]{2,1,0:T(1,128)} %tile_id.1, s32[1,1,32]{2,1,0:T(1,128)} %tile_n.1), custom_call_target="tpu_custom_call" | custom-call | tf_op jit(solution)/shard_map/step/pallas_call | solution.py:469
  40.5 1.1 %copy.8 = f32[3,8,16,1024]{3,2,1,0:T(8,128)} copy(f32[3,8,16,1024]{3,2,1,0:T(8,128)S(1)} %step.1) | data formatting | bytes 3145728

commit v5 on v4

--- a/solution.py
+++ b/solution.py
@@ -10,21 +10,23 @@
 TS = 128
 DIFFUSION = 0.15
 MESH = pl.DeviceIdType.MESH
+LEVELS = 32767.0
+SMALLEST = 1e-30
 CHIP_X = 4
 
 AROUND = (3, 4, 5)
 AROUND_LAST = 5
-THROUGH = (0, 1, 2, 6)
+THROUGH = (0, 1, 2)
 STRAIGHT = (0, 7, 5, 1, 2, 6)
 
 
 def kernel(
     vort, rotor, cour, tiles, tile_id, tile_n, out,
-    vbuf, cbuf, rbuf, rin, comb, src, vup,
-    relay_a, relay_b, relay_p, edge_f, edge_s, edge_r, edge_out, edge_in,
+    vbuf, cbuf, rbuf, rin, comb, src, code_out, code_in, scale_out, scale_in,
+    relay_a, relay_b, relay_p, edge_f, edge_s, edge_r, edge_out, edge_in, seam_v, seam_r,
     tbuf, idbuf, cntbuf, sbuf, trecv, tsib, tmat,
     lsem, r_send, r_recv, a_send, a_recv, b_send, b_recv, c_send,
-    p_recv, q_send, h_send, h_recv, e_send, e_recv, t_send, t_recv, up_sem, down_sem, seam_sem,
+    p_recv, q_send, h_send, h_recv, e_send, e_recv, t_send, t_recv, up_sem, down_sem, seam_sem, seam_next,
 ):
     n_azi, n_ra = lax.axis_size("azi"), lax.axis_size("ra")
     n_y = n_azi // CHIP_X
@@ -131,14 +133,41 @@
         i = AROUND.index(k)
         return remote(row(relay_b, i), row(rin, k), c_send.at[i], r_recv.at[k], device)
 
-    low_edge = remote(row(vort, 0), vup, h_send.at[0], h_recv.at[0], preceding)
-    high_edge = remote(row(comb, rows_az), row(comb, 0), h_send.at[1], h_recv.at[1], following)
+    def halo(side):
+        to = (preceding, following)[side]
+        return (
+            remote(code_out.at[side], code_in.at[side], h_send.at[side], h_recv.at[side], to),
+            remote(
+                scale_out.at[side], scale_in.at[side], h_send.at[3 + side], h_recv.at[3 + side], to
+            ),
+        )
+
+    def encode(side, values):
+        scale_lane = lax.broadcasted_iota(jnp.int32, (rows_rad, TS), 1)
+        scales = jnp.zeros((rows_rad, TS), jnp.float32)
+        for c in range(3):
+            value = values(c)
+            largest = jnp.max(jnp.abs(value), axis=1, keepdims=True)
+            largest = jnp.maximum(largest, SMALLEST)
+            code = jnp.round(value * (LEVELS / largest))
+            code_out[side, c] = code.astype(jnp.int32).astype(jnp.int16)
+            scales = jnp.where(scale_lane == c, largest * (1.0 / LEVELS), scales)
+        scale_out[side] = scales
+        for copy in halo(side):
+            copy.start()
+
+    def decode(side, c):
+        return code_in[side, c].astype(jnp.int32).astype(jnp.float32) * scale_in[side, :, c : c + 1]
+
     edges = remote(edge_s, edge_r, h_send.at[2], h_recv.at[2], following)
 
     def radial(side, device):
         return remote(
             edge_out.at[side], edge_in.at[side], e_send.at[side], e_recv.at[side], device
         )
+
+    seam_own = remote(edge_out.at[0], seam_v, e_send.at[2], e_recv.at[2], higher)
+    seam_turned = remote(edge_s, seam_r, e_send.at[3], e_recv.at[3], ((j + 1) % n_azi, r + 1))
 
     capacity = tbuf.shape[0] // n_ra
     group = 2 * capacity
@@ -165,19 +194,6 @@
     around(3).start()
     start_row(5)
     around(4).start()
-
-    loads[0].wait()
-    for c in range(3):
-        for k in range(rows_az):
-            whole = rbuf[c, k].astype(jnp.float32)
-            edge_f[c, k : k + 1] = whole[:1]
-            edge_f[c, rows_az + k : rows_az + k + 1] = whole[rows_rad - 1 :]
-    edge_s[...] = edge_f[...].astype(jnp.bfloat16)
-    edges.start()
-    start_row(1)
-    low_edge.start()
-    start_row(2)
-    start_row(6)
 
     pl.when(z_low)(lambda: pl.semaphore_wait(up_sem, 1))
     pl.when(z_high)(
@@ -223,6 +239,35 @@
             for d in range(1, n_chip):
                 tile_copy(d).start()
 
+    send_tiles(n_z - 2, n_z - 1)
+
+    loads[0].wait()
+    for c in range(3):
+        for k in range(rows_az):
+            whole = rbuf[c, k].astype(jnp.float32)
+            edge_f[c, k : k + 1] = whole[:1]
+            edge_f[c, rows_az + k : rows_az + k + 1] = whole[rows_rad - 1 :]
+    edge_s[...] = edge_f[...].astype(jnp.bfloat16)
+    @pl.when(seam_high)
+    def _():
+        pl.semaphore_wait(seam_sem, 1)
+        pl.semaphore_signal(seam_next, inc=1, device_id=preceding, device_id_type=MESH)
+        pl.semaphore_wait(seam_next, 1)
+        seam_turned.start()
+
+    edges.start()
+    loads[1].wait()
+    for c in range(3):
+        for k in range(rows_az):
+            edge_out[1, c, k : k + 1] = vbuf[c, k, :1]
+            edge_out[0, c, k : k + 1] = vbuf[c, k, rows_rad - 1 :]
+
+    pl.when(seam_high)(lambda: seam_own.start())
+    start_row(1)
+    encode(0, lambda c: vbuf[c, 0])
+    start_row(2)
+    start_row(6)
+
     def take(k):
         straight(k).wait_recv()
         for c in range(3):
@@ -246,13 +291,6 @@
         around_on(k, down_x).wait_recv()
         around_end(k, at(0, y + 1) if k == AROUND_LAST else down_x).start()
 
-    send_tiles(n_z - 2, n_z - 1)
-    loads[1].wait()
-    for c in range(3):
-        for k in range(rows_az):
-            edge_out[1, c, k : k + 1] = vbuf[c, k, :1]
-            edge_out[0, c, k : k + 1] = vbuf[c, k, rows_rad - 1 :]
-
     @pl.when(jnp.logical_not(has_low))
     def _():
         edge_in[0] = jnp.zeros_like(edge_in[0])
@@ -261,26 +299,27 @@
     def _():
         edge_in[1] = jnp.zeros_like(edge_in[1])
 
+    send_tiles(n_z - 4, n_z - 3)
     relay_through(0)
     relay_first(3)
     take(7)
-    high_edge.start()
-    send_tiles(n_z - 4, n_z - 3)
+    encode(1, lambda c: comb[c, rows_az])
+    send_tiles(2, n_z - 5)
     relay_through(1)
     pl.when(x == 2)(lambda: relay_first(5))
     relay_first(4)
     relay_through(2)
+    send_tiles(0, 1)
     edges.wait_recv()
+    pl.when(seam_high)(lambda: seam_own.wait_send())
     for c in range(3):
         arrived = edge_r[c].astype(jnp.float32)
         edge_out[1, c] += arrived[:rows_az]
         edge_out[0, c] += arrived[rows_az:]
     in_run_low = jnp.logical_and(has_low, jnp.logical_not(seam_low))
-    pl.when(seam_high)(lambda: pl.semaphore_wait(seam_sem, 1))
-    pl.when(has_high)(lambda: radial(0, higher).start())
+    in_run_high = jnp.logical_and(has_high, jnp.logical_not(seam_high))
+    pl.when(in_run_high)(lambda: radial(0, higher).start())
     pl.when(in_run_low)(lambda: radial(1, lower).start())
-    send_tiles(0, n_z - 5)
-    relay_through(6)
     relay_second(3)
     pl.when(x == 1)(lambda: relay_second(5))
     relay_second(4)
@@ -362,11 +401,20 @@
                 ]
 
     loads[5].wait()
-    low_edge.wait_recv()
+    for copy in (*halo(0), *halo(1)):
+        copy.wait_recv()
     for c in range(3):
-        comb[c, rows_az + 1] = vup[c, 0] + rbuf[c, 0].astype(jnp.float32)
-    high_edge.wait_recv()
-    pl.when(has_low)(lambda: radial(0, (j, r)).wait_recv())
+        comb[c, rows_az + 1] = decode(0, c) + rbuf[c, 0].astype(jnp.float32)
+        comb[c, 0] = decode(1, c)
+    pl.when(in_run_low)(lambda: radial(0, (j, r)).wait_recv())
+
+    @pl.when(seam_low)
+    def _():
+        seam_own.wait_recv()
+        seam_turned.wait_recv()
+        for c in range(3):
+            edge_in[0, c] = seam_v[c] + seam_r[c].astype(jnp.float32)[rows_az:]
+
     pl.when(has_high)(lambda: radial(1, (j, r)).wait_recv())
     stencil(0)
     take(3)
@@ -399,10 +447,11 @@
         for k in THROUGH:
             through_on(k).wait_send()
 
-    low_edge.wait_send()
-    high_edge.wait_send()
+    for copy in (*halo(0), *halo(1)):
+        copy.wait_send()
     edges.wait_send()
-    pl.when(has_high)(lambda: radial(0, (j, r)).wait_send())
+    pl.when(in_run_high)(lambda: radial(0, (j, r)).wait_send())
+    pl.when(seam_high)(lambda: seam_turned.wait_send())
     pl.when(has_low)(lambda: radial(1, (j, r)).wait_send())
     for d in range(1, n_chip):
         tile_copy(d).wait_send()
@@ -416,7 +465,6 @@
     n_ra = lax.axis_size("ra")
     n_chip = n_ra // 2
     group = slots // n_chip
-    one_row = (3, 1, rows_rad, cells_ax)
 
     def relay(n):
         return pltpu.VMEM((3, n, rows_rad, cells_ax), jnp.bfloat16)
@@ -430,7 +478,10 @@
         pltpu.VMEM(shape, jnp.bfloat16),
         pltpu.VMEM((3, rows_az + 2, rows_rad, cells_ax), jnp.float32),
         pltpu.VMEM(shape, jnp.float32),
-        pltpu.VMEM(one_row, jnp.float32),
+        pltpu.VMEM((2, 3, rows_rad, cells_ax), jnp.int16),
+        pltpu.VMEM((2, 3, rows_rad, cells_ax), jnp.int16),
+        pltpu.VMEM((2, rows_rad, TS), jnp.float32),
+        pltpu.VMEM((2, rows_rad, TS), jnp.float32),
         relay(around),
         relay(around),
         relay(through),
@@ -439,6 +490,8 @@
         pltpu.VMEM((3, 2 * rows_az, cells_ax), jnp.bfloat16),
         pltpu.VMEM((2, 3, rows_az, cells_ax), jnp.float32),
         pltpu.VMEM((2, 3, rows_az, cells_ax), jnp.float32),
+        pltpu.VMEM((3, rows_az, cells_ax), jnp.float32),
+        pltpu.VMEM((3, 2 * rows_az, cells_ax), jnp.bfloat16),
         pltpu.VMEM((slots, width), jnp.float32),
         pltpu.VMEM((1, slots), jnp.int32),
         pltpu.VMEM((1, n_ra), jnp.int32),
@@ -456,12 +509,13 @@
         dma((around,)),
         dma((through,)),
         dma((through,)),
-        dma((3,)),
-        dma((3,)),
-        dma((2,)),
-        dma((2,)),
+        dma((5,)),
+        dma((5,)),
+        dma((4,)),
+        dma((4,)),
         dma((n_chip,)),
         dma((n_chip,)),
+        pltpu.SemaphoreType.REGULAR,
         pltpu.SemaphoreType.REGULAR,
         pltpu.SemaphoreType.REGULAR,
         pltpu.SemaphoreType.REGULAR,

time: 41.7 us -> 38.4 us (0.921)
  the two profiles are of different devices: /device:TPU:57 before, /device:TPU:30 now
where the time goes in v5:
time: 38.4 us; the launch traced here: 38.3 us
  Pallas kernels  37.2 us (97%)
  local copies, waits for them, and re-layouts  1.15 us (3%)
    pallas_call x1, Pallas kernels, body(): pl.pallas_call(kernel, name='step', out_shape=pltpu.VMEM(shape, jnp.float...  37.2 us
    unnamed x1, local copies, waits for them, and re-layouts  1.15 us

profile of v5, /device:TPU:30, one launch (start us, length us, event | category | flops | bytes accessed | tf_op | source)
XLA Modules:
  0.0 38.3 jit_solution(5776542858581246313)
XLA Ops:
  0.0 37.2 %step.1 = f32[3,8,16,1024]{3,2,1,0:T(8,128)S(1)} custom-call(f32[3,8,16,1024]{3,2,1,0:T(8,128)} %vort.1, bf16[3,8,16,1024]{3,2,1,0:T(8,128)(2,1)} %rotor.1, bf16[3,8,16,1024]{3,2,1,0:T(8,128)(2,1)} %cour.1, f32[1,1,128,384]{3,2,1,0:T(8,128)} %tiles.1, s32[1,1,128]{2,1,0:T(1,128)} %tile_id.1, s32[1,1,32]{2,1,0:T(1,128)} %tile_n.1), custom_call_target="tpu_custom_call" | custom-call | tf_op jit(solution)/shard_map/step/pallas_call | solution.py:523
  37.2 1.1 %copy.8 = f32[3,8,16,1024]{3,2,1,0:T(8,128)} copy(f32[3,8,16,1024]{3,2,1,0:T(8,128)S(1)} %step.1) | data formatting | bytes 3145728

commit v6 on v5

--- a/solution.py
+++ b/solution.py
@@ -10,6 +10,7 @@
 TS = 128
 DIFFUSION = 0.15
 MESH = pl.DeviceIdType.MESH
+SOURCE_AFTER = (0, 1, 2, 3, 4)
 LEVELS = 32767.0
 SMALLEST = 1e-30
 CHIP_X = 4
@@ -26,7 +27,7 @@
     relay_a, relay_b, relay_p, edge_f, edge_s, edge_r, edge_out, edge_in, seam_v, seam_r,
     tbuf, idbuf, cntbuf, sbuf, trecv, tsib, tmat,
     lsem, r_send, r_recv, a_send, a_recv, b_send, b_recv, c_send,
-    p_recv, q_send, h_send, h_recv, e_send, e_recv, t_send, t_recv, up_sem, down_sem, seam_sem, seam_next,
+    p_recv, q_send, h_send, h_recv, e_send, e_recv, t_send, t_recv, up_sem, down_sem, above_sem, seam_sem, seam_next,
 ):
     n_azi, n_ra = lax.axis_size("azi"), lax.axis_size("ra")
     n_y = n_azi // CHIP_X
@@ -95,11 +96,9 @@
         greet(at(1, y + n_y - 1))
 
     pl.when(z_high)(lambda: greet(above))
-    pl.when(z_low)(lambda: greet(below))
-    pl.when(near_low)(lambda: greet(lower))
     pl.when(near_high)(lambda: greet(higher))
     others = 5 + 3 * first.astype(jnp.int32) + (x == 1).astype(jnp.int32)
-    for near in (z_high, z_low, near_low, near_high):
+    for near in (z_low, near_low):
         others = others + near.astype(jnp.int32)
 
     pl.semaphore_wait(bar, others)
@@ -195,10 +194,16 @@
     start_row(5)
     around(4).start()
 
+    pl.when(z_low)(
+        lambda: pl.semaphore_signal(above_sem, inc=1, device_id=below, device_id_type=MESH)
+    )
     pl.when(z_low)(lambda: pl.semaphore_wait(up_sem, 1))
-    pl.when(z_high)(
-        lambda: pl.semaphore_signal(up_sem, inc=1, device_id=above, device_id_type=MESH)
-    )
+
+    @pl.when(z_high)
+    def _():
+        pl.semaphore_wait(above_sem, 1)
+        pl.semaphore_signal(up_sem, inc=1, device_id=above, device_id_type=MESH)
+
     @pl.when(jnp.logical_not(z_high))
     def _():
         for d in range(1, n_z):
@@ -291,7 +296,10 @@
         around_on(k, down_x).wait_recv()
         around_end(k, at(0, y + 1) if k == AROUND_LAST else down_x).start()
 
-    @pl.when(jnp.logical_not(has_low))
+    in_run_low = jnp.logical_and(has_low, jnp.logical_not(seam_low))
+    in_run_high = jnp.logical_and(has_high, jnp.logical_not(seam_high))
+
+    @pl.when(jnp.logical_not(in_run_low))
     def _():
         edge_in[0] = jnp.zeros_like(edge_in[0])
 
@@ -316,8 +324,6 @@
         arrived = edge_r[c].astype(jnp.float32)
         edge_out[1, c] += arrived[:rows_az]
         edge_out[0, c] += arrived[rows_az:]
-    in_run_low = jnp.logical_and(has_low, jnp.logical_not(seam_low))
-    in_run_high = jnp.logical_and(has_high, jnp.logical_not(seam_high))
     pl.when(in_run_high)(lambda: radial(0, higher).start())
     pl.when(in_run_low)(lambda: radial(1, lower).start())
     relay_second(3)
@@ -325,7 +331,6 @@
     relay_second(4)
     take(0)
     take(1)
-    take(5)
 
     @pl.when(seam_low)
     def _():
@@ -343,7 +348,7 @@
     inverse = 1.0 / (0.5 + (position + 0.5) / (rows_rad * n_ra))
     inverse_sq = inverse * inverse
 
-    def stencil(k):
+    def stencil(k, with_source):
         v0 = cbuf[0, k].astype(jnp.float32)
         v1 = cbuf[1, k].astype(jnp.float32)
         v2 = cbuf[2, k].astype(jnp.float32)
@@ -362,7 +367,9 @@
             down = jnp.where(radial_row == 0, edge_in[0, c, k : k + 1], down)
             right = jnp.where(axial == cells_ax - 1, 0.0, pltpu.roll(f, cells_ax - 1, 1))
             left = jnp.where(axial == 0, 0.0, pltpu.roll(f, 1, 1))
-            total = middle * f + src[c, k]
+            total = middle * f
+            if with_source:
+                total = total + src[c, k]
             total = total + DIFFUSION * ((up + down) + (right + left))
             total = total + rad * (up - down) - axi * (right - left)
             total = total + azi_even * (nxt + prv) - azi_odd * (nxt - prv)
@@ -371,6 +378,24 @@
             elif c == 1:
                 total = total - (0.5 * turn) * f + turn * (comb[0, k + 2] - comb[0, k])
             out[c, k] = total
+
+    loads[5].wait()
+    take(3)
+    pl.when(in_run_low)(lambda: radial(0, (j, r)).wait_recv())
+    pl.when(has_high)(lambda: radial(1, (j, r)).wait_recv())
+    take(2)
+    stencil(1, False)
+    stencil(2, False)
+    for copy in (*halo(0), *halo(1)):
+        copy.wait_recv()
+    for c in range(3):
+        comb[c, rows_az + 1] = decode(0, c) + rbuf[c, 0].astype(jnp.float32)
+        comb[c, 0] = decode(1, c)
+    stencil(0, False)
+    take(5)
+    take(4)
+    stencil(3, False)
+    stencil(4, False)
 
     exchange.wait_recv()
     keep = (slot % group) // capacity == core
@@ -396,38 +421,28 @@
         )
         for b in range(per_row):
             for c in range(3):
-                src[c, a, :, b * TS : (b + 1) * TS] = placed[
-                    b * rows_rad : (b + 1) * rows_rad, c * TS : (c + 1) * TS
-                ]
-
-    loads[5].wait()
-    for copy in (*halo(0), *halo(1)):
-        copy.wait_recv()
-    for c in range(3):
-        comb[c, rows_az + 1] = decode(0, c) + rbuf[c, 0].astype(jnp.float32)
-        comb[c, 0] = decode(1, c)
-    pl.when(in_run_low)(lambda: radial(0, (j, r)).wait_recv())
+                block = placed[b * rows_rad : (b + 1) * rows_rad, c * TS : (c + 1) * TS]
+                if a in SOURCE_AFTER:
+                    out[c, a, :, b * TS : (b + 1) * TS] += block
+                else:
+                    src[c, a, :, b * TS : (b + 1) * TS] = block
+
+    take(6)
+    stencil(7, True)
+    stencil(5, True)
+    stencil(6, True)
 
     @pl.when(seam_low)
     def _():
         seam_own.wait_recv()
         seam_turned.wait_recv()
+        edge_inverse = inverse[:1]
         for c in range(3):
-            edge_in[0, c] = seam_v[c] + seam_r[c].astype(jnp.float32)[rows_az:]
-
-    pl.when(has_high)(lambda: radial(1, (j, r)).wait_recv())
-    stencil(0)
-    take(3)
-    take(4)
-    stencil(4)
-    take(2)
-    stencil(1)
-    stencil(2)
-    stencil(3)
-    take(6)
-    stencil(7)
-    stencil(5)
-    stencil(6)
+            arrived = seam_v[c] + seam_r[c].astype(jnp.float32)[rows_az:]
+            for k in range(rows_az):
+                v0 = cbuf[0, k].astype(jnp.float32)[:1]
+                weight = DIFFUSION - (0.25 * DIFFUSION) * edge_inverse + 0.5 * v0
+                out[c, k, :1] += weight * arrived[k : k + 1]
 
     for k in STRAIGHT:
         if k != AROUND_LAST:
@@ -519,6 +534,7 @@
         pltpu.SemaphoreType.REGULAR,
         pltpu.SemaphoreType.REGULAR,
         pltpu.SemaphoreType.REGULAR,
+        pltpu.SemaphoreType.REGULAR,
     ]
     return pl.pallas_call(
         kernel,

time: 38.4 us -> 37.3 us (0.971)
  the two profiles are of different devices: /device:TPU:30 before, /device:TPU:449 now
where the time goes in v6:
time: 37.3 us; the launch traced here: 37.2 us
  Pallas kernels  36 us (97%)
  local copies, waits for them, and re-layouts  1.15 us (3%)
    pallas_call x1, Pallas kernels, body(): pl.pallas_call(kernel, name='step', out_shape=pltpu.VMEM(shape, jnp.float...  36 us
    unnamed x1, local copies, waits for them, and re-layouts  1.15 us

profile of v6, /device:TPU:449, one launch (start us, length us, event | category | flops | bytes accessed | tf_op | source)
XLA Modules:
  0.0 37.2 jit_solution(17800225883956291973)
XLA Ops:
  0.0 36.0 %step.1 = f32[3,8,16,1024]{3,2,1,0:T(8,128)S(1)} custom-call(f32[3,8,16,1024]{3,2,1,0:T(8,128)} %vort.1, bf16[3,8,16,1024]{3,2,1,0:T(8,128)(2,1)} %rotor.1, bf16[3,8,16,1024]{3,2,1,0:T(8,128)(2,1)} %cour.1, f32[1,1,128,384]{3,2,1,0:T(8,128)} %tiles.1, s32[1,1,128]{2,1,0:T(1,128)} %tile_id.1, s32[1,1,32]{2,1,0:T(1,128)} %tile_n.1), custom_call_target="tpu_custom_call" | custom-call | tf_op jit(solution)/shard_map/step/pallas_call | solution.py:539
  36.0 1.1 %copy.8 = f32[3,8,16,1024]{3,2,1,0:T(8,128)} copy(f32[3,8,16,1024]{3,2,1,0:T(8,128)S(1)} %step.1) | data formatting | bytes 3145728

commit v7 on v6

--- a/solution.py
+++ b/solution.py
@@ -10,7 +10,7 @@
 TS = 128
 DIFFUSION = 0.15
 MESH = pl.DeviceIdType.MESH
-SOURCE_AFTER = (0, 1, 2, 3, 4)
+SOURCE_AFTER = (0, 1, 2, 7)
 LEVELS = 32767.0
 SMALLEST = 1e-30
 CHIP_X = 4
@@ -24,7 +24,7 @@
 def kernel(
     vort, rotor, cour, tiles, tile_id, tile_n, out,
     vbuf, cbuf, rbuf, rin, comb, src, code_out, code_in, scale_out, scale_in,
-    relay_a, relay_b, relay_p, edge_f, edge_s, edge_r, edge_out, edge_in, seam_v, seam_r,
+    relay_a, relay_b, relay_p, edge_f, edge_s, edge_r, edge_out, edge_in, seam_v, seam_s, seam_r,
     tbuf, idbuf, cntbuf, sbuf, trecv, tsib, tmat,
     lsem, r_send, r_recv, a_send, a_recv, b_send, b_recv, c_send,
     p_recv, q_send, h_send, h_recv, e_send, e_recv, t_send, t_recv, up_sem, down_sem, above_sem, seam_sem, seam_next,
@@ -63,6 +63,33 @@
     def row(ref, k):
         return ref.at[:, pl.ds(k, 1)]
 
+    bar = pltpu.get_barrier_semaphore()
+
+    def greet(device):
+        pl.semaphore_signal(bar, inc=1, device_id=device, device_id_type=MESH)
+
+    greet(following)
+    greet(preceding)
+    greet(sibling)
+    greet((j, (r + n_ra // 2) % n_ra))
+    pl.when(last)(lambda: greet(up_x))
+    pl.when(first)(lambda: greet(down_x))
+    pl.when(x == 2)(lambda: greet(at(1, y + 1)))
+    pl.when(x == 1)(lambda: greet(at(2, y + n_y - 1)))
+    pl.when(x == 1)(lambda: greet(at(0, y + 1)))
+
+    @pl.when(first)
+    def _():
+        greet(up_y)
+        greet(down_y)
+        greet(at(1, y + n_y - 1))
+
+    pl.when(z_high)(lambda: greet(above))
+    pl.when(near_high)(lambda: greet(higher))
+    others = 5 + 3 * first.astype(jnp.int32) + (x == 1).astype(jnp.int32)
+    for near in (z_low, near_low):
+        others = others + near.astype(jnp.int32)
+
     loads = [
         local(rotor, rbuf, 0),
         local(vort, vbuf, 1),
@@ -73,33 +100,6 @@
     ]
     for load in loads:
         load.start()
-
-    bar = pltpu.get_barrier_semaphore()
-
-    def greet(device):
-        pl.semaphore_signal(bar, inc=1, device_id=device, device_id_type=MESH)
-
-    greet(following)
-    greet(preceding)
-    greet(sibling)
-    greet((j, (r + n_ra // 2) % n_ra))
-    pl.when(last)(lambda: greet(up_x))
-    pl.when(first)(lambda: greet(down_x))
-    pl.when(x == 2)(lambda: greet(at(1, y + 1)))
-    pl.when(x == 1)(lambda: greet(at(2, y + n_y - 1)))
-    pl.when(x == 1)(lambda: greet(at(0, y + 1)))
-
-    @pl.when(first)
-    def _():
-        greet(up_y)
-        greet(down_y)
-        greet(at(1, y + n_y - 1))
-
-    pl.when(z_high)(lambda: greet(above))
-    pl.when(near_high)(lambda: greet(higher))
-    others = 5 + 3 * first.astype(jnp.int32) + (x == 1).astype(jnp.int32)
-    for near in (z_low, near_low):
-        others = others + near.astype(jnp.int32)
 
     pl.semaphore_wait(bar, others)
 
@@ -166,7 +166,7 @@
         )
 
     seam_own = remote(edge_out.at[0], seam_v, e_send.at[2], e_recv.at[2], higher)
-    seam_turned = remote(edge_s, seam_r, e_send.at[3], e_recv.at[3], ((j + 1) % n_azi, r + 1))
+    seam_turned = remote(seam_s, seam_r, e_send.at[3], e_recv.at[3], ((j + 1) % n_azi, r + 1))
 
     capacity = tbuf.shape[0] // n_ra
     group = 2 * capacity
@@ -246,6 +246,11 @@
 
     send_tiles(n_z - 2, n_z - 1)
 
+    @pl.when(seam_high)
+    def _():
+        pl.semaphore_wait(seam_sem, 1)
+        pl.semaphore_signal(seam_next, inc=1, device_id=preceding, device_id_type=MESH)
+
     loads[0].wait()
     for c in range(3):
         for k in range(rows_az):
@@ -255,8 +260,8 @@
     edge_s[...] = edge_f[...].astype(jnp.bfloat16)
     @pl.when(seam_high)
     def _():
-        pl.semaphore_wait(seam_sem, 1)
-        pl.semaphore_signal(seam_next, inc=1, device_id=preceding, device_id_type=MESH)
+        high = [edge_f[c, rows_az:] for c in range(3)]
+        seam_s[...] = jnp.concatenate([*high, high[0]], axis=0).astype(jnp.bfloat16)
         pl.semaphore_wait(seam_next, 1)
         seam_turned.start()
 
@@ -392,10 +397,8 @@
         comb[c, rows_az + 1] = decode(0, c) + rbuf[c, 0].astype(jnp.float32)
         comb[c, 0] = decode(1, c)
     stencil(0, False)
-    take(5)
-    take(4)
-    stencil(3, False)
-    stencil(4, False)
+    take(6)
+    stencil(7, False)
 
     exchange.wait_recv()
     keep = (slot % group) // capacity == core
@@ -427,18 +430,21 @@
                 else:
                     src[c, a, :, b * TS : (b + 1) * TS] = block
 
-    take(6)
-    stencil(7, True)
+    take(5)
+    stencil(6, True)
+    take(4)
+    stencil(3, True)
+    stencil(4, True)
     stencil(5, True)
-    stencil(6, True)
 
     @pl.when(seam_low)
     def _():
         seam_own.wait_recv()
         seam_turned.wait_recv()
         edge_inverse = inverse[:1]
+        turned = seam_r[...].astype(jnp.float32)
         for c in range(3):
-            arrived = seam_v[c] + seam_r[c].astype(jnp.float32)[rows_az:]
+            arrived = seam_v[c] + turned[c * rows_az : (c + 1) * rows_az]
             for k in range(rows_az):
                 v0 = cbuf[0, k].astype(jnp.float32)[:1]
                 weight = DIFFUSION - (0.25 * DIFFUSION) * edge_inverse + 0.5 * v0
@@ -506,7 +512,8 @@
         pltpu.VMEM((2, 3, rows_az, cells_ax), jnp.float32),
         pltpu.VMEM((2, 3, rows_az, cells_ax), jnp.float32),
         pltpu.VMEM((3, rows_az, cells_ax), jnp.float32),
-        pltpu.VMEM((3, 2 * rows_az, cells_ax), jnp.bfloat16),
+        pltpu.VMEM((4 * rows_az, cells_ax), jnp.bfloat16),
+        pltpu.VMEM((4 * rows_az, cells_ax), jnp.bfloat16),
         pltpu.VMEM((slots, width), jnp.float32),
         pltpu.VMEM((1, slots), jnp.int32),
         pltpu.VMEM((1, n_ra), jnp.int32),

time: 37.3 us -> 36.7 us (0.984)
  Pallas kernels: 36 us -> 35.4 us
    pallas_call x1, Pallas kernels: 36 us -> 35.4 us  [body(): pl.pallas_call(kernel, name='step', out_shape=pltpu.VMEM(shape, jnp.float...]
where the time goes in v7:
time: 36.7 us; the launch traced here: 36.5 us
  Pallas kernels  35.4 us (96%)
  local copies, waits for them, and re-layouts  1.15 us (3%)
    pallas_call x1, Pallas kernels, body(): pl.pallas_call(kernel, name='step', out_shape=pltpu.VMEM(shape, jnp.float...  35.4 us
    unnamed x1, local copies, waits for them, and re-layouts  1.15 us

profile of v7, /device:TPU:449, one launch (start us, length us, event | category | flops | bytes accessed | tf_op | source)
XLA Modules:
  0.0 36.5 jit_solution(12238003431423681441)
XLA Ops:
  0.0 35.4 %step.1 = f32[3,8,16,1024]{3,2,1,0:T(8,128)S(1)} custom-call(f32[3,8,16,1024]{3,2,1,0:T(8,128)} %vort.1, bf16[3,8,16,1024]{3,2,1,0:T(8,128)(2,1)} %rotor.1, bf16[3,8,16,1024]{3,2,1,0:T(8,128)(2,1)} %cour.1, f32[1,1,128,384]{3,2,1,0:T(8,128)} %tiles.1, s32[1,1,128]{2,1,0:T(1,128)} %tile_id.1, s32[1,1,32]{2,1,0:T(1,128)} %tile_n.1), custom_call_target="tpu_custom_call" | custom-call | tf_op jit(solution)/shard_map/step/pallas_call | solution.py:546
  35.4 1.1 %copy.8 = f32[3,8,16,1024]{3,2,1,0:T(8,128)} copy(f32[3,8,16,1024]{3,2,1,0:T(8,128)S(1)} %step.1) | data formatting | bytes 3145728
